TPU v7x, 128 devices: a whole 4x4x4 slice. The times are simulated.
128 devices in a mesh: dp: 64 (over z, y, x_hi, core), seq: 2 (over x_lo).
Axes of the slice: x: 4 (x_hi: 2, x_lo: 2; x = x_hi * 2 + x_lo), y: 4, z: 4, core: 2. Of those that a mesh axis runs over, the one named last changes fastest.
Arguments:
- inputs: bfloat16 [128, 512, 768], P('dp', 'seq'), may hold values from -6 to 6
- memory: bfloat16 [128, 256, 768], P('dp', 'seq'), may hold values from -6 to 6
- cotangent: bfloat16 [128, 512, 768], P('dp', 'seq'), may hold values from -6 to 6
- seg_ids: int32 [128, 512], P('dp', 'seq'), may hold values from 0 to 7, as said below
- mem_seg: int32 [128, 256], P('dp', 'seq'), may hold values from 0 to 7, as said below
- tasks: int32 [128], P('dp'), may hold values from 0 to 7
- self_qkv: bfloat16 [768, 2304], P('dp'), may hold values from -0.21875 to 0.21875
- self_out: bfloat16 [768, 768], P('dp'), may hold values from -1.25 to 1.25
- cross_query: bfloat16 [768, 768], P('dp'), may hold values from -0.21875 to 0.21875
- cross_kv: bfloat16 [768, 1536], P('dp'), may hold values from -0.21875 to 0.21875
- cross_out: bfloat16 [768, 768], P('dp'), may hold values from -1.25 to 1.25
- ff_in: bfloat16 [768, 3072], P('dp'), may hold values from -0.21875 to 0.21875
- ff_out: bfloat16 [3072, 768], P('dp'), may hold values from -0.109375 to 0.109375
- gen_down: bfloat16 [64, 18432], P(None, 'dp'), may hold values from -0.0390625 to 0.0390625
- gen_up: bfloat16 [64, 18432], P(None, 'dp'), may hold values from -0.21875 to 0.21875
- gen_gain: bfloat16 [64, 768], P(None, 'dp'), may hold values from -0.375 to 0.375
- task_table: float32 [8, 64], replicated, may hold values from -6 to 6
- place_table: float32 [3, 64], replicated, may hold values from -6 to 6
- proj_in: float32 [128, 128], replicated, may hold values from -0.5 to 0.5
- proj_out: float32 [128, 64], replicated, may hold values from -0.5 to 0.5
Outputs:
- mixed: bfloat16 [128, 512, 768], P('dp', 'seq')
- grad_input: float32 [128, 512, 768], P('dp', 'seq')
- grad_memory: float32 [128, 256, 768], P('dp', 'seq')
- grad_self_qkv: float32 [768, 2304], P('dp')
- grad_self_out: float32 [768, 768], P('dp')
- grad_cross_query: float32 [768, 768], P('dp')
- grad_cross_kv: float32 [768, 1536], P('dp')
- grad_cross_out: float32 [768, 768], P('dp')
- grad_ff_in: float32 [768, 3072], P('dp')
- grad_ff_out: float32 [3072, 768], P('dp')
- grad_gen_down: float32 [64, 18432], P(None, 'dp')
- grad_gen_up: float32 [64, 18432], P(None, 'dp')
- grad_gen_gain: float32 [64, 768], P(None, 'dp')
- task_embedding_gradient: float32 [8, 64], replicated
- grad_place_table: float32 [3, 64], replicated
- grad_proj_in: float32 [128, 128], replicated
- output_projection_gradient: float32 [128, 64], replicated
Inputs may be any that keep to these rules, and one draw needn't show every extreme that they name: `seg_ids`: within each pack the ids never fall from row to row and every id occurs. `mem_seg`: within each pack the ids never fall from row to row and every id occurs.
All inputs are finite; a program needn't handle non-finite values.
Results may differ from a plain program's by a relative error of at most 0.03.
The roundings to bfloat16 on the way count: a program that leaves them out, or rounds other values in their place, can miss the bound.
Values may be sent and summed in bfloat16 or wider, within the bound.
No kernel may reach another device: no remote copies, remote signals or barrier semaphores. Data moves between devices by JAX's collectives and lax.ppermute only.
A program may use at most 256 MiB of HBM per device.

v0:
```python
from functools import partial
import math

import jax
import jax.numpy as jnp
from jax import lax
from jax.sharding import PartitionSpec as P

D = 768
HEADS = 12
HD = 64
R = 24


epsilon = 1e-06
masked_out = -1e30
highest_precision = lax.Precision.HIGHEST


def passed_along(value, axis, steps):
    count = lax.axis_size(axis)
    first, last = (max(0, -steps), min(count, count - steps))
    return lax.ppermute(value, axis, [(source, source + steps) for source in range(first, last)])


def norm_apply(resid, gains):
    inverse = lax.rsqrt(jnp.mean(resid * resid, axis=-1, keepdims=True) + epsilon)
    return resid * inverse * gains[:, None, :]


def norm_back(resid, gains, grad_norm):
    _, pull_back = jax.vjp(norm_apply, resid, gains)
    return pull_back(grad_norm)


def gelu_back(pre_act, grad_act):
    _, pull_back = jax.vjp(jax.nn.gelu, pre_act)
    return pull_back(grad_act)[0]


def project(left, weight):
    return jnp.einsum("prd,de->pre", left, weight, preferred_element_type=jnp.float32)


def project_back(grad_out, weight):
    return jnp.einsum("pre,de->prd", grad_out, weight, preferred_element_type=jnp.float32)


def weight_grad(left, grad_out):
    return jnp.einsum("prd,pre->de", left, grad_out, preferred_element_type=jnp.float32)


def split_heads(matrix):
    return matrix.reshape(matrix.shape[0], HEADS, HD)


def head_scores(queries, keys, mask):
    raw = jnp.einsum(
        "qhd,khd->hqk", split_heads(queries), split_heads(keys), preferred_element_type=jnp.float32
    ) * (1.0 / math.sqrt(HD))
    return jnp.where(mask[None], raw, masked_out)


def attend_forward(queries, keys, values, mask):
    scores = head_scores(queries, keys, mask)
    maximum = jnp.max(scores, axis=-1, keepdims=True)
    exponent = jnp.exp(scores - maximum)
    total = jnp.sum(exponent, axis=-1, keepdims=True)
    probs_low = (exponent / total).astype(jnp.bfloat16)
    attn_out = jnp.einsum(
        "hqk,khd->qhd", probs_low, split_heads(values), preferred_element_type=jnp.float32
    )
    return (
        attn_out.reshape(queries.shape[0], D).astype(jnp.bfloat16),
        (maximum + jnp.log(total))[..., 0],
    )


def attend_backward(queries, keys, values, mask, log_total, grad_out):
    scores = head_scores(queries, keys, mask)
    softmax_prob = jnp.exp(scores - log_total[..., None])
    grad_prob = jnp.einsum(
        "qhd,khd->hqk",
        split_heads(grad_out),
        split_heads(values),
        preferred_element_type=jnp.float32,
    )
    grad_score = softmax_prob * (
        grad_prob - jnp.sum(grad_prob * softmax_prob, axis=-1, keepdims=True)
    )
    grad_score = grad_score.astype(jnp.bfloat16)
    score_scale = 1.0 / math.sqrt(HD)
    grad_query = (
        jnp.einsum(
            "hqk,khd->qhd", grad_score, split_heads(keys), preferred_element_type=jnp.float32
        )
        * score_scale
    )
    grad_key = (
        jnp.einsum(
            "hqk,qhd->khd", grad_score, split_heads(queries), preferred_element_type=jnp.float32
        )
        * score_scale
    )
    grad_value = jnp.einsum(
        "hqk,qhd->khd",
        softmax_prob.astype(jnp.bfloat16),
        split_heads(grad_out),
        preferred_element_type=jnp.float32,
    )
    key_rows = keys.shape[0]
    return (
        grad_query.reshape(queries.shape[0], D),
        jnp.concatenate([grad_key.reshape(key_rows, D), grad_value.reshape(key_rows, D)], axis=1),
    )


def adapter_forward(branch, down_gen, up_gen):
    branch_low = branch.astype(jnp.bfloat16)
    pre_act = jnp.einsum("prd,pdk->prk", branch_low, down_gen, preferred_element_type=jnp.float32)
    hidden_state = jax.nn.gelu(pre_act).astype(jnp.bfloat16)
    layer_result = jnp.einsum(
        "prk,pkd->prd", hidden_state, up_gen, preferred_element_type=jnp.float32
    )
    return (layer_result, (branch_low, pre_act, hidden_state))


def adapter_backward(grad_resid, kept, down_gen, up_gen):
    branch_low, pre_act, hidden_state = kept
    grad_adapt = grad_resid.astype(jnp.bfloat16)
    grad_up = jnp.einsum(
        "prk,prd->pkd", hidden_state, grad_adapt, preferred_element_type=jnp.float32
    )
    grad_hidden = jnp.einsum("prd,pkd->prk", grad_adapt, up_gen, preferred_element_type=jnp.float32)
    grad_pre = gelu_back(pre_act, grad_hidden).astype(jnp.bfloat16)
    grad_down = jnp.einsum("prd,prk->pdk", branch_low, grad_pre, preferred_element_type=jnp.float32)
    grad_branch = grad_resid + jnp.einsum(
        "prk,pdk->prd", grad_pre, down_gen, preferred_element_type=jnp.float32
    )
    return (
        grad_branch.astype(jnp.bfloat16),
        grad_down.astype(jnp.bfloat16),
        grad_up.astype(jnp.bfloat16),
    )


def hyper_codes(onehot, task_table, place_table, proj_in, proj_out):
    embedding = jnp.dot(onehot, task_table, precision=highest_precision)
    pack_count = onehot.shape[0]
    places = place_table.shape[0]
    width = task_table.shape[1]
    joined_in = jnp.concatenate(
        [
            jnp.broadcast_to(embedding[:, None, :], (pack_count, places, width)),
            jnp.broadcast_to(place_table[None], (pack_count, places, width)),
        ],
        axis=-1,
    )
    hidden_state = jax.nn.gelu(
        jnp.einsum("pai,ih->pah", joined_in, proj_in, precision=highest_precision)
    )
    return jnp.einsum("pah,ht->pat", hidden_state, proj_out, precision=highest_precision)


def shards(
    inputs,
    memory,
    cotangent,
    seg_ids,
    mem_seg,
    tasks,
    self_qkv,
    self_out,
    cross_query,
    cross_kv,
    cross_out,
    ff_in,
    ff_out,
    gen_down,
    gen_up,
    gen_gain,
    task_table,
    place_table,
    proj_in,
    proj_out,
):
    seq_index = lax.axis_index("seq")
    pack_count = inputs.shape[0]
    row_count = inputs.shape[1]
    (
        full_self_qkv,
        full_self_out,
        full_query,
        full_mem_kv,
        full_cross_out,
        full_ff_in,
        full_ff_out,
        full_down,
        full_up,
        full_gain,
    ) = (
        lax.all_gather(self_qkv, "dp", axis=0, tiled=True),
        lax.all_gather(self_out, "dp", axis=0, tiled=True),
        lax.all_gather(cross_query, "dp", axis=0, tiled=True),
        lax.all_gather(cross_kv, "dp", axis=0, tiled=True),
        lax.all_gather(cross_out, "dp", axis=0, tiled=True),
        lax.all_gather(ff_in, "dp", axis=0, tiled=True),
        lax.all_gather(ff_out, "dp", axis=0, tiled=True),
        lax.all_gather(gen_down, "dp", axis=1, tiled=True),
        lax.all_gather(gen_up, "dp", axis=1, tiled=True),
        lax.all_gather(gen_gain, "dp", axis=1, tiled=True),
    )
    onehot = (tasks[:, None] == jnp.arange(task_table.shape[0], dtype=jnp.int32)[None, :]).astype(
        jnp.float32
    )
    codes, hyper_pull = jax.vjp(
        partial(hyper_codes, onehot), task_table, place_table, proj_in, proj_out
    )
    codes_low = codes.astype(jnp.bfloat16)
    down_all = (
        jnp.einsum("pat,tc->pac", codes_low, full_down, preferred_element_type=jnp.float32)
        .astype(jnp.bfloat16)
        .reshape(pack_count, 3, D, R)
    )
    up_all = (
        jnp.einsum("pat,tc->pac", codes_low, full_up, preferred_element_type=jnp.float32)
        .astype(jnp.bfloat16)
        .reshape(pack_count, 3, R, D)
    )
    gain_all = 1.0 + jnp.einsum(
        "pat,tc->pac", codes_low, full_gain, preferred_element_type=jnp.float32
    )
    seg_float = seg_ids.astype(jnp.bfloat16)
    mem_float = mem_seg.astype(jnp.bfloat16)
    resid_zero = inputs.astype(jnp.float32)
    normed_one = norm_apply(resid_zero, gain_all[:, 0]).astype(jnp.bfloat16)
    self_proj = project(normed_one, full_self_qkv).astype(jnp.bfloat16)
    mem_rows, mem_docs, all_docs = (
        lax.all_gather(memory, "seq", axis=1, tiled=True),
        lax.all_gather(mem_float, "seq", axis=1, tiled=True),
        lax.all_gather(seg_float, "seq", axis=1, tiled=True),
    )
    mem_keys = project(mem_rows, full_mem_kv).astype(jnp.bfloat16)
    own_kv = self_proj[..., D:]
    remote_kv = passed_along(own_kv, "seq", 1)
    remote_docs = lax.dynamic_slice_in_dim(
        all_docs, jnp.maximum(seq_index - 1, 0) * row_count, row_count, 1
    )
    positions = jnp.arange(row_count)
    causal = positions[None, :] <= positions[:, None]
    local_mask = (seg_float[:, :, None] == seg_float[:, None, :]) & causal[None]
    remote_mask = (seg_float[:, :, None] == remote_docs[:, None, :]) & (seq_index > 0)
    self_mask = jnp.concatenate([remote_mask, local_mask], axis=2)
    cross_mask = seg_float[:, :, None] == mem_docs[:, None, :]
    self_kv = jnp.concatenate([remote_kv, own_kv], axis=1)
    self_queries = self_proj[..., :D]
    self_keys = self_kv[..., :D]
    self_values = self_kv[..., D:]
    attended_one, total_one = lax.map(
        lambda packed: attend_forward(*packed), (self_queries, self_keys, self_values, self_mask)
    )
    branch_one = project(attended_one, full_self_out)
    adapt_one, kept_one = adapter_forward(branch_one, down_all[:, 0], up_all[:, 0])
    resid_one = resid_zero + branch_one + adapt_one
    normed_two = norm_apply(resid_one, gain_all[:, 1]).astype(jnp.bfloat16)
    cross_queries = project(normed_two, full_query).astype(jnp.bfloat16)
    mem_k = mem_keys[..., :D]
    mem_v = mem_keys[..., D:]
    attended_two, total_two = lax.map(
        lambda packed: attend_forward(*packed), (cross_queries, mem_k, mem_v, cross_mask)
    )
    branch_two = project(attended_two, full_cross_out)
    adapt_two, kept_two = adapter_forward(branch_two, down_all[:, 1], up_all[:, 1])
    resid_two = resid_one + branch_two + adapt_two
    normed_three = norm_apply(resid_two, gain_all[:, 2]).astype(jnp.bfloat16)
    ff_pre = project(normed_three, full_ff_in)
    ff_hidden = jax.nn.gelu(ff_pre).astype(jnp.bfloat16)
    branch_three = project(ff_hidden, full_ff_out)
    adapt_three, kept_three = adapter_forward(branch_three, down_all[:, 2], up_all[:, 2])
    resid_three = resid_two + branch_three + adapt_three
    mixed = resid_three.astype(jnp.bfloat16)
    grad_three = cotangent.astype(jnp.float32)
    branch_grad, down_three, up_three = adapter_backward(
        grad_three, kept_three, down_all[:, 2], up_all[:, 2]
    )
    grad_ff_out = weight_grad(ff_hidden, branch_grad)
    hidden_grad = project_back(branch_grad, full_ff_out)
    pre_grad = gelu_back(ff_pre, hidden_grad).astype(jnp.bfloat16)
    grad_ff_in = weight_grad(normed_three, pre_grad)
    resid_grad, gain_three = norm_back(
        resid_two, gain_all[:, 2], project_back(pre_grad, full_ff_in)
    )
    grad_two = grad_three + resid_grad
    branch_grad, down_two, up_two = adapter_backward(
        grad_two, kept_two, down_all[:, 1], up_all[:, 1]
    )
    grad_cross_out = weight_grad(attended_two, branch_grad)
    out_grad = project_back(branch_grad, full_cross_out).astype(jnp.bfloat16)
    query_grad, mem_kv_grad = lax.map(
        lambda packed: attend_backward(*packed),
        (cross_queries, mem_k, mem_v, cross_mask, total_two, out_grad),
    )
    query_low = query_grad.astype(jnp.bfloat16)
    grad_cross_query = weight_grad(normed_two, query_low)
    own_mem_grad = lax.psum_scatter(
        mem_kv_grad.astype(jnp.bfloat16), "seq", scatter_dimension=1, tiled=True
    )
    grad_cross_kv = weight_grad(memory, own_mem_grad)
    grad_memory = project_back(own_mem_grad, full_mem_kv)
    resid_grad, gain_two = norm_back(resid_one, gain_all[:, 1], project_back(query_low, full_query))
    grad_one = grad_two + resid_grad
    branch_grad, down_one, up_one = adapter_backward(
        grad_one, kept_one, down_all[:, 0], up_all[:, 0]
    )
    grad_self_out = weight_grad(attended_one, branch_grad)
    out_grad = project_back(branch_grad, full_self_out).astype(jnp.bfloat16)
    query_grad, self_kv_grad = lax.map(
        lambda packed: attend_backward(*packed),
        (self_queries, self_keys, self_values, self_mask, total_one, out_grad),
    )
    returned_kv = passed_along(self_kv_grad[:, :row_count].astype(jnp.bfloat16), "seq", -1).astype(
        jnp.float32
    )
    own_kv_grad = self_kv_grad[:, row_count:] + returned_kv
    proj_grad = jnp.concatenate([query_grad, own_kv_grad], axis=2).astype(jnp.bfloat16)
    grad_self_qkv = weight_grad(normed_one, proj_grad)
    resid_grad, gain_one = norm_back(
        resid_zero, gain_all[:, 0], project_back(proj_grad, full_self_qkv)
    )
    grad_input = grad_one + resid_grad
    down_grads = jnp.stack([down_one, down_two, down_three], axis=1).reshape(pack_count, 3, D * R)
    up_grads = jnp.stack([up_one, up_two, up_three], axis=1).reshape(pack_count, 3, R * D)
    gain_grads = jnp.stack([gain_one, gain_two, gain_three], axis=1)
    grad_gen_gain = jnp.einsum(
        "pat,pac->tc", codes_low.astype(jnp.float32), gain_grads, precision=highest_precision
    )
    grad_codes = (
        jnp.einsum("pac,tc->pat", down_grads, full_down, preferred_element_type=jnp.float32)
        + jnp.einsum("pac,tc->pat", up_grads, full_up, preferred_element_type=jnp.float32)
        + jnp.einsum(
            "pac,tc->pat", gain_grads, full_gain.astype(jnp.float32), precision=highest_precision
        )
    )
    table_grad, place_grad, proj_in_grad, proj_out_grad = hyper_pull(grad_codes)
    table_sum, place_sum, proj_in_sum, proj_out_sum = lax.psum(
        (table_grad, place_grad, proj_in_grad, proj_out_grad), ("dp", "seq")
    )
    grad_gen_down = jnp.einsum(
        "pat,pac->tc", codes_low, down_grads, preferred_element_type=jnp.float32
    )
    grad_gen_up = jnp.einsum("pat,pac->tc", codes_low, up_grads, preferred_element_type=jnp.float32)
    part_down, part_up = (
        lax.psum_scatter(grad_gen_down, "dp", scatter_dimension=1, tiled=True),
        lax.psum_scatter(grad_gen_up, "dp", scatter_dimension=1, tiled=True),
    )
    sum_down, sum_up = (
        lax.psum(part_down.astype(jnp.bfloat16), "seq").astype(jnp.float32),
        lax.psum(part_up.astype(jnp.bfloat16), "seq").astype(jnp.float32),
    )
    (
        part_qkv,
        part_self_out,
        part_query,
        part_mem_kv,
        part_cross_out,
        part_ff_in,
        part_ff_out,
        part_gain,
    ) = (
        lax.psum_scatter(grad_self_qkv, "dp", scatter_dimension=0, tiled=True),
        lax.psum_scatter(grad_self_out, "dp", scatter_dimension=0, tiled=True),
        lax.psum_scatter(grad_cross_query, "dp", scatter_dimension=0, tiled=True),
        lax.psum_scatter(grad_cross_kv, "dp", scatter_dimension=0, tiled=True),
        lax.psum_scatter(grad_cross_out, "dp", scatter_dimension=0, tiled=True),
        lax.psum_scatter(grad_ff_in, "dp", scatter_dimension=0, tiled=True),
        lax.psum_scatter(grad_ff_out, "dp", scatter_dimension=0, tiled=True),
        lax.psum_scatter(grad_gen_gain, "dp", scatter_dimension=1, tiled=True),
    )
    sum_qkv, sum_self_out, sum_query, sum_mem_kv, sum_cross_out, sum_ff_in, sum_ff_out, sum_gain = (
        lax.psum(part_qkv.astype(jnp.bfloat16), "seq").astype(jnp.float32),
        lax.psum(part_self_out.astype(jnp.bfloat16), "seq").astype(jnp.float32),
        lax.psum(part_query.astype(jnp.bfloat16), "seq").astype(jnp.float32),
        lax.psum(part_mem_kv.astype(jnp.bfloat16), "seq").astype(jnp.float32),
        lax.psum(part_cross_out.astype(jnp.bfloat16), "seq").astype(jnp.float32),
        lax.psum(part_ff_in.astype(jnp.bfloat16), "seq").astype(jnp.float32),
        lax.psum(part_ff_out.astype(jnp.bfloat16), "seq").astype(jnp.float32),
        lax.psum(part_gain.astype(jnp.bfloat16), "seq").astype(jnp.float32),
    )
    return (
        mixed,
        grad_input,
        grad_memory,
        sum_qkv,
        sum_self_out,
        sum_query,
        sum_mem_kv,
        sum_cross_out,
        sum_ff_in,
        sum_ff_out,
        sum_down,
        sum_up,
        sum_gain,
        table_sum,
        place_sum,
        proj_in_sum,
        proj_out_sum,
    )


def solution(mesh):
    in_specs = (
        P("dp", "seq", None),
        P("dp", "seq", None),
        P("dp", "seq", None),
        P("dp", "seq"),
        P("dp", "seq"),
        P("dp"),
        P("dp", None),
        P("dp", None),
        P("dp", None),
        P("dp", None),
        P("dp", None),
        P("dp", None),
        P("dp", None),
        P(None, "dp"),
        P(None, "dp"),
        P(None, "dp"),
        P(),
        P(),
        P(),
        P(),
    )
    out_specs = (
        P("dp", "seq", None),
        P("dp", "seq", None),
        P("dp", "seq", None),
        P("dp", None),
        P("dp", None),
        P("dp", None),
        P("dp", None),
        P("dp", None),
        P("dp", None),
        P("dp", None),
        P(None, "dp"),
        P(None, "dp"),
        P(None, "dp"),
        P(),
        P(),
        P(),
        P(),
    )
    return jax.shard_map(shards, mesh=mesh, in_specs=in_specs, out_specs=out_specs, check_vma=False)
```

profile of v0, /device:TPU:1, one launch (start us, length us, event | category | flops | bytes accessed | tf_op | source)
XLA Modules:
  0.0 2182.6 jit_solution(2179381762043302096)
XLA Ops:
  23.0 101.7 %all-gather = bf16[64,12,64]{2,1,0:T(8,128)(2,1)S(1)} all-gather(bf16[1,12,64]{2,1,0:T(8,128)(2,1)} %bitcast.465), channel_id=1, replica_groups=mesh['dp'=64,'seq'=2] {'dp'}, dimensions={0}, use_global_device_ids=true | all-gather | bytes 99840 | tf_op jit(solution)/shard_map/all_gather | solution.py:211
  146.8 40.0 %all_gather.45 = bf16[2,256,768]{2,1,0:T(8,128)(2,1)} all-gather(bf16[2,128,768]{2,1,0:T(8,128)(2,1)S(1)} %copy-done.49), channel_id=1, replica_groups=mesh['dp'=64,'seq'=2] {'seq'}, dimensions={1}, use_global_device_ids=true | all-gather | bytes 1179648 | tf_op jit(solution)/shard_map/all_gather | solution.py:239
  189.9 35.7 %all-gather.31.cloned.1.call-done = bf16[64,12,768]{2,1,0:T(8,128)(2,1)} async-done(((bf16[1,12,768]{2,1,0:T(8,128)(2,1)}), bf16[64,12,768]{2,1,0:T(8,128)(2,1)}) %all-gather.31.cloned.1.call-update) | async-done | bytes 1179664 | tf_op jit(solution)/shard_map/all_gather | solution.py:204
  228.8 63.7 %all-gather.33.cloned.1.call-done = bf16[64,12,768]{2,1,0:T(8,128)(2,1)} async-done(((bf16[1,12,768]{2,1,0:T(8,128)(2,1)}), bf16[64,12,768]{2,1,0:T(8,128)(2,1)}) %all-gather.33.cloned.1.call-update) | async-done | bytes 1179664 | tf_op jit(solution)/shard_map/all_gather | solution.py:206
  295.6 66.5 %all-gather.25.cloned.1.call-done = bf16[64,288,64]{1,2,0:T(8,128)(2,1)} async-done(((bf16[1,288,64]{1,2,0:T(8,128)(2,1)}), bf16[64,288,64]{1,2,0:T(8,128)(2,1)}) %all-gather.25.cloned.1.call-update) | async-done | bytes 2359312 | tf_op jit(solution)/shard_map/all_gather | solution.py:209
  373.9 58.7 %all-gather.27.cloned.1.call-done = bf16[64,288,64]{1,2,0:T(8,128)(2,1)} async-done(((bf16[1,288,64]{1,2,0:T(8,128)(2,1)}), bf16[64,288,64]{1,2,0:T(8,128)(2,1)}) %all-gather.27.cloned.1.call-update) | async-done | bytes 2359312 | tf_op jit(solution)/shard_map/all_gather | solution.py:210
  446.7 56.5 %all-gather.29.cloned.1.call-done = bf16[64,12,1536]{2,1,0:T(8,128)(2,1)} async-done(((bf16[1,12,1536]{2,1,0:T(8,128)(2,1)}), bf16[64,12,1536]{2,1,0:T(8,128)(2,1)}) %all-gather.29.cloned.1.call-update) | async-done | bytes 2359312 | tf_op jit(solution)/shard_map/all_gather | solution.py:205
  529.6 18.1 while.48
  571.9 8.6 all-gather.35.cloned.1.call-done
  580.4 7.5 reshape.327
  595.0 60.4 %all-gather.19.cloned.1.call-done = bf16[3072,768]{1,0:T(8,128)(2,1)} async-done(((bf16[48,768]{1,0:T(8,128)(2,1)}), bf16[3072,768]{1,0:T(8,128)(2,1)}) %all-gather.19.cloned.1.call-update) | async-done | bytes 4718608 | tf_op jit(solution)/shard_map/all_gather | solution.py:208
  655.3 7.6 fusion.39
  681.4 20.8 while.50
  752.2 46.9 %while.51 = (s32[]{:T(128)}, bf16[2,256,768]{2,1,0:T(8,128)(2,1)}, f32[2,512,1536]{2,1,0:T(8,128)}, bf16[2,512,768]{1,2,0:T(8,128)(2,1)}, pred[2,256,512]{2,1,0:...) while((s32[]{:T(128)}, bf16[2,256,768]{2,1,0:T(8,128)(2,1)}, ...), condition=%wide.region_18.19_spmd, body=%wide.region_16.18_spmd.sunk | while | flops 1031795712 | bytes 81350792 | solution.py:317
  803.9 9.8 convolution_bitcast_fusion.3
  827.8 20.9 collective-permute-done.1
  861.6 378.4 %fusion.133 = (f32[16,2304]{1,0:T(8,128)S(1)}, f32[16,768]{1,0:T(8,128)}, f32[16,768]{1,0:T(8,128)}, f32[16,768]{1,0:T(8,128)}, f32[64,16]{0,1:T(8,128)}, /*index=5*/f32[16,3072]{1,0:T(8,128)S(1)}) fusion(f32[768,2304]{1,0:T(8,128)} %convolution_bitcast_fusion.2, f32[768,768]{1,0:T(8,128)} %convolution_bitcast_fusion.8, ...), kind=kCustom, calls=%all-reduce-scatter.6 | all-reduce-scatter fusion | flops 7929857 | bytes 24285696
  1399.3 7.2 collective-permute-start.22
  1448.1 12.5 concatenate.30
  1520.1 8.8 concatenate.25
  1541.6 38.1 %concatenate.29 = bf16[268,3072]{1,0:T(8,128)(2,1)} concatenate(bf16[12,3072]{1,0:T(8,128)(2,1)S(1)} %collective-permute-done.81, bf16[16,3072]{1,0:T(8,128)(2,1)S(1)} %collective-permute-done.80, bf16[16,3072]{1,0:T(8,128)(2,1)S(1)} %collective-permute-done.79, bf16[16,3072]{1,0:T(8,128)(2,1)S(1)} %collective-permute-done.78, bf16[16,3072]{1,0:T(8,128)(2,1)S(1)} %collective-permute-done.77, ...), dimensions={0} | concatenate | bytes 3391488
  1586.0 365.8 %all-reduce.27 = bf16[768,1536]{0,1:T(8,128)(2,1)S(1)} all-reduce(f32[768,1536]{0,1:T(8,128)} %convolution_bitcast_fusion.5), channel_id=6, replica_groups=mesh['dp'=64,'seq'=2] {'dp'}, use_global_device_ids=true, to_apply=%region_27.28.clone | all-reduce | flops 1179648 | bytes 7077888
  1960.7 70.0 %all-reduce.13 = (f32[8,64]{1,0:T(8,128)}, f32[3,64]{1,0:T(4,128)}, f32[128,64]{0,1:T(8,128)}) all-reduce(f32[8,64]{1,0:T(8,128)S(1)} %copy-done.139, f32[3,64]{1,0:T(4,128)S(1)} %copy-done.134, f32[128,64]{0,1:T(8,128)S(1)} %convolution_bitcast_fusion.12), channel_id=1, replica_groups=mesh['dp'=64,'seq'=2] {'dp','seq'}, use_global_device_ids=true, to_apply=%region_45.46 | all-reduce | flops 8896 | bytes 71168 | tf_op jit(solution)/shard_map/psum | solution.py:345
  2048.8 125.6 %all-reduce.22.cloned.1.call-done = f32[128,128]{1,0:T(8,128)} async-done(((f32[128,128]{1,0:T(8,128)}), f32[128,128]{1,0:T(8,128)}) %all-reduce.22.cloned.1.call-update) | async-done | bytes 65552 | tf_op jit(solution)/shard_map/psum | solution.py:345
  (807 shorter events, 626.7 us)
Async XLA Ops:
  7.2 121.6 %all-gather.21.cloned.1.call-start = ((), (), s32[]{:S(2)}) async-start(), calls=%async_computation.7 | async-start | bytes 4792320 | tf_op jit(solution)/shard_map/all_gather | solution.py:202
  7.9 178.8 %all-gather.23.cloned.1.call-start = ((), (), s32[]{:S(2)}) async-start(), calls=%async_computation.8 | async-start | bytes 1597440 | tf_op jit(solution)/shard_map/all_gather | solution.py:203
  8.7 216.9 %all-gather.31.cloned.1.call-start = ((), (), s32[]{:S(2)}) async-start(), calls=%async_computation.12 | async-start | bytes 1597440 | tf_op jit(solution)/shard_map/all_gather | solution.py:204
  9.4 283.1 %all-gather.33.cloned.1.call-start = ((), (), s32[]{:S(2)}) async-start(), calls=%async_computation.13 | async-start | bytes 1597440 | tf_op jit(solution)/shard_map/all_gather | solution.py:206
  10.0 352.1 %all-gather.25.cloned.1.call-start = ((), (), s32[]{:S(2)}) async-start(), calls=%async_computation.9 | async-start | bytes 3194880 | tf_op jit(solution)/shard_map/all_gather | solution.py:209
  10.6 422.0 %all-gather.27.cloned.1.call-start = ((), (), s32[]{:S(2)}) async-start(), calls=%async_computation.10 | async-start | bytes 3194880 | tf_op jit(solution)/shard_map/all_gather | solution.py:210
  11.2 492.0 %all-gather.29.cloned.1.call-start = ((), (), s32[]{:S(2)}) async-start(), calls=%async_computation.11 | async-start | bytes 3194880 | tf_op jit(solution)/shard_map/all_gather | solution.py:205
  11.9 568.5 %all-gather.35.cloned.1.call-start = ((), (), s32[]{:S(2)}) async-start(), calls=%async_computation.14 | async-start | bytes 6389760 | tf_op jit(solution)/shard_map/all_gather | solution.py:207
  12.7 642.7 %all-gather.19.cloned.1.call-start = ((), (), s32[]{:S(2)}) async-start(), calls=%async_computation.4 | async-start | bytes 4792320 | tf_op jit(solution)/shard_map/all_gather | solution.py:208
  13.4 1566.3 %reduce-scatter.26.cloned.1.call-start = ((), (), s32[]{:S(2)}) async-start(), calls=%async_computation.15 | async-start | bytes 2359296
  142.1 377.6 %collective-permute-start = (bf16[2,256,1536]{2,1,0:T(8,128)(2,1)}, bf16[2,256,1536]{2,1,0:T(8,128)(2,1)}, u32[]{:S(2)}, u32[]{:S(2)}) collective-permute-start(bf16[2,256,1536]{2,1,0:T(8,128)(2,1)} %slice.79), channel_id=1, source_target_pairs={{0,1},{2,3},{4,5},{6,7},{8,9},{10,11},{12,13},{14,15},{16,17},{18,... | collective-permute-start | bytes 4718600 | tf_op jit(solution)/shard_map/ppermute | solution.py:23
  707.4 1245.4 %reduce-scatter.30.cloned.1.call-start = ((), (), s32[]{:S(2)}) async-start(), calls=%async_computation.17 | async-start | bytes 9584640
  725.1 1229.4 %reduce-scatter.28.cloned.1.call-start = ((), (), s32[]{:S(2)}) async-start(), calls=%async_computation.16 | async-start | bytes 9584640
  751.5 1206.2 %reduce-scatter.24.cloned.1.call-start = ((), (), s32[]{:S(2)}) async-start(), calls=%async_computation.5 | async-start | bytes 9584640 | tf_op jit(solution)/shard_map/reduce_scatter | solution.py:376
  802.5 46.3 %collective-permute-start.1 = (bf16[2,256,1536]{2,1,0:T(8,128)(2,1)}, bf16[2,256,1536]{2,1,0:T(8,128)(2,1)}, u32[]{:S(2)}, u32[]{:S(2)}) collective-permute-start(bf16[2,256,1536]{2,1,0:T(8,128)(2,1)} %slice.132), channel_id=1, source_target_pairs={{1,0},{3,2},{5,4},{7,6},{9,8},{11,10},{13,12},{15,14},{17,16},{19,... | collective-permute-start | bytes 4718600 | tf_op jit(solution)/shard_map/ppermute | solution.py:23
  813.8 1220.2 %all-reduce.24.cloned.1.call-start = ((), (), s32[]{:S(2)}) async-start(), calls=%async_computation.18 | async-start | bytes 1286144 | tf_op jit(solution)/shard_map/psum | solution.py:380
  1258.5 26.4 %collective-permute-start.87 = (bf16[64,16]{0,1:T(8,128)(2,1)S(1)}, bf16[64,16]{0,1:T(8,128)(2,1)}, u32[]{:S(2)}, u32[]{:S(2)}) collective-permute-start(bf16[64,16]{0,1:T(8,128)(2,1)S(1)} %convert.217), channel_id=1, source_target_pairs={{0,12},{2,14},{4,16},{6,18},{8,20},{10,22},{12,24},{14,26},{16,28}... | collective-permute-start | bytes 6152
  1284.8 44.4 %collective-permute-start.51 = (bf16[16,768]{1,0:T(8,128)(2,1)}, bf16[16,768]{1,0:T(8,128)(2,1)}, u32[]{:S(2)}, u32[]{:S(2)}) collective-permute-start(bf16[16,768]{1,0:T(8,128)(2,1)} %convert.214), channel_id=1, source_target_pairs={{0,4},{2,6},{4,8},{6,10},{8,12},{10,14},{12,16},{14,18},{16,20},{1... | collective-permute-start | bytes 73736
  1288.1 43.3 %collective-permute-start.52 = (bf16[16,768]{1,0:T(8,128)(2,1)}, bf16[16,768]{1,0:T(8,128)(2,1)}, u32[]{:S(2)}, u32[]{:S(2)}) collective-permute-start(bf16[16,768]{1,0:T(8,128)(2,1)} %convert.214), channel_id=1, source_target_pairs={{0,6},{2,8},{4,10},{6,12},{8,14},{10,16},{12,18},{14,20},{16,22},{... | collective-permute-start | bytes 73736
  1432.0 28.6 %collective-permute-start.4 = (bf16[16,2304]{1,0:T(8,128)(2,1)S(1)}, bf16[16,2304]{1,0:T(8,128)(2,1)S(1)}, u32[]{:S(2)}, u32[]{:S(2)}) collective-permute-start(bf16[16,2304]{1,0:T(8,128)(2,1)S(1)} %convert.213), channel_id=1, source_target_pairs={{0,6},{2,8},{4,10},{6,12},{8,14},{10,16},{12,18},{14,20},{16,22},{... | collective-permute-start | bytes 221192
  1433.3 28.7 %collective-permute-start.5 = (bf16[16,2304]{1,0:T(8,128)(2,1)S(1)}, bf16[16,2304]{1,0:T(8,128)(2,1)S(1)}, u32[]{:S(2)}, u32[]{:S(2)}) collective-permute-start(bf16[16,2304]{1,0:T(8,128)(2,1)S(1)} %convert.213), channel_id=1, source_target_pairs={{0,8},{2,10},{4,12},{6,14},{8,16},{10,18},{12,20},{14,22},{16,24},... | collective-permute-start | bytes 221192
  1435.5 30.2 %collective-permute-start.6 = (bf16[16,2304]{1,0:T(8,128)(2,1)S(1)}, bf16[16,2304]{1,0:T(8,128)(2,1)S(1)}, u32[]{:S(2)}, u32[]{:S(2)}) collective-permute-start(bf16[16,2304]{1,0:T(8,128)(2,1)S(1)} %convert.213), channel_id=1, source_target_pairs={{0,10},{2,12},{4,14},{6,16},{8,18},{10,20},{12,22},{14,24},{16,26}... | collective-permute-start | bytes 221192
  1956.1 89.6 %all-reduce.26.cloned.1.call-start = ((), (), s32[]{:S(2)}) async-start(), calls=%async_computation.19 | async-start | bytes 344064 | tf_op jit(solution)/shard_map/psum | solution.py:385
  1959.3 215.1 %all-reduce.22.cloned.1.call-start = ((), (), s32[]{:S(2)}) async-start(), calls=%async_computation.6 | async-start | bytes 131072 | tf_op jit(solution)/shard_map/psum | solution.py:345
  (246 other events, 5709.7 us)
Sparse Core Ops, SparseCore 0:
  11.1 76.7 all-gather.20
  90.9 67.2 all-gather.22
  161.3 64.3 all-gather.30
  228.5 63.8 all-gather.32
  295.4 66.6 all-gather.24
  365.1 67.4 all-gather.26
  435.6 67.4 all-gather.28
  506.2 74.1 all-gather.34
  583.5 71.7 all-gather.18
  707.6 26.5 reduce-scatter.25
  740.9 185.5 reduce-scatter.29
  932.1 192.9 reduce-scatter.27
  1131.8 173.9 reduce-scatter.23
  1956.2 40.6 all-reduce.23
  1999.9 29.3 all-reduce.25
  2035.2 139.1 all-reduce.21
where the time goes:
time: 2200 us; the launch traced here: 2180 us
  blocking collectives  963 us (44%)
  waiting for transfers between devices  503 us (23%)
  starting transfers between devices  248 us (11%)
  local copies, waits for them, and re-layouts  243 us (11%)
  matrix products  164 us (7%)
  other arithmetic  42.4 us (2%)
    unnamed x2, blocking collectives  744 us
    unnamed x99, starting transfers between devices  242 us
    unnamed x311, local copies, waits for them, and re-layouts  147 us
    psum x1, waiting for transfers between devices, shards(): lax.psum((table_grad, place_grad, proj_in_grad, proj_out_grad), ('dp', 's...  126 us
    all_gather x1, blocking collectives, shards(): lax.all_gather(gen_gain, 'dp', axis=1, tiled=True)  102 us
    psum x1, blocking collectives, shards(): lax.psum((table_grad, place_grad, proj_in_grad, proj_out_grad), ('dp', 's...  70 us
    all_gather x1, waiting for transfers between devices, shards(): lax.all_gather(gen_down, 'dp', axis=1, tiled=True)  66.5 us
    all_gather x1, waiting for transfers between devices, shards(): lax.all_gather(cross_out, 'dp', axis=0, tiled=True)  63.7 us
  transfers between devices with their start and end apart: 114, of which 10 were waited for; matrix products, arithmetic and copies ran while one was open for 35% of the time, Pallas kernels for 0%

commit v1 on v0

v1 whole, which is shorter than its diff:
```python
from functools import partial
import math

import jax
import jax.numpy as jnp
from jax import lax
from jax.experimental import pallas as pl
from jax.experimental.pallas import tpu as pltpu
from jax.sharding import PartitionSpec as P

D = 768
HEADS = 12
HD = 64
PAIRS = HEADS // 2
FF = 3072
R = 24
NTASK = 8
TE = 64
WIDE = NTASK * R
PLACE = 256
ROWS = 256

epsilon = 1e-06
masked_out = -1e30
highest_precision = lax.Precision.HIGHEST
low = jnp.bfloat16
full = jnp.float32
scale = 1.0 / math.sqrt(HD)


def mm(left, right):
    return jnp.dot(left, right, preferred_element_type=full)


def swap(value, axis, mask):
    count = lax.axis_size(axis)
    return lax.ppermute(value, axis, [(i, i ^ mask) for i in range(count)])


def group_exchange(value):
    me = lax.axis_index("dp") % 4
    got = [lax.dynamic_index_in_dim(value, me, 0, keepdims=False)]
    for step in (1, 2, 3):
        got.append(swap(lax.dynamic_index_in_dim(value, me ^ step, 0, keepdims=False), "dp", step))
    got = jnp.stack(got)
    return jnp.take(got, jnp.arange(4) ^ me, axis=0)


def from_quarters(rows48):
    cols = rows48.shape[1]
    pieces = group_exchange(rows48.reshape(4, 12, cols))
    return pieces.transpose(1, 0, 2).reshape(12, 4 * cols)


WEIGHTS = (
    ("self_out", 0, 768),
    ("query", 768, 768),
    ("cross_out", 1536, 768),
    ("mem_kv", 2304, 1536),
    ("down", 3840, 512),
    ("ff_in", 4608, 3072),
)
QUARTER = 1920
FF_ROWS = 128
EARLY = 640


def early_gather(block):
    along_x = jnp.stack([block, swap(block, "dp", 2)])
    along_z = jnp.stack([along_x] + [swap(along_x, "dp", step << 4) for step in (1, 2, 3)])
    return jnp.stack([along_z] + [swap(along_z, "dp", step << 2) for step in (1, 2, 3)])


def unpack_early(own, other):
    dp = lax.axis_index("dp")

    def body(place_ref, own_ref, other_ref, qkv, down):
        for mine in range(4):

            @pl.when(place_ref[2] == mine)
            def _():
                for q in range(4):
                    step = q ^ mine
                    src = (own_ref, other_ref)[step % 2]
                    if q < 3:
                        qkv[0, :, EARLY * q : EARLY * (q + 1)] = src[0, 0, step // 2]
                    else:
                        qkv[0, :, EARLY * q :] = src[0, 0, step // 2, :, : 2304 - 3 * EARLY]
                        down[0] = src[0, 0, step // 2, :, 2304 - 3 * EARLY :]

    def place_of(g, place):
        return ((g % 4) ^ place[1], (g // 4) ^ place[0], 0, 0, 0)

    return pl.pallas_call(
        body,
        grid_spec=pltpu.PrefetchScalarGridSpec(
            num_scalar_prefetch=1,
            grid=(16,),
            in_specs=[pl.BlockSpec((1, 1, 2, 48, EARLY), place_of)] * 2,
            out_specs=[
                pl.BlockSpec((1, 48, 2304), lambda g, place: (g, 0, 0)),
                pl.BlockSpec((1, 48, PLACE), lambda g, place: (g, 0, 0)),
            ],
        ),
        out_shape=[jax.ShapeDtypeStruct((16, 48, 2304), low), jax.ShapeDtypeStruct((16, 48, PLACE), low)],
        compiler_params=pltpu.CompilerParams(vmem_limit_bytes=6 * 2**20),
        name="unpack_early",
    )(jnp.stack([dp // 16, (dp // 4) % 4, dp % 4]).astype(jnp.int32), own, other)


def up_tiles():
    for block in (0, 1):
        for j in range(3):
            k, half = divmod(3 * block + j, 2)
            for piece in range(3):
                lane, row = divmod(3 * j + piece, 6)
                yield block, 8 * row, 128 * lane, 8 * k, 384 * half + 128 * piece


def unpack(gathered):
    def body(src, *outs):
        for (_, start, width), out in zip(WEIGHTS, outs):
            for q in range(4):
                first, last = max(start, q * QUARTER), min(start + width, (q + 1) * QUARTER)
                if first < last:
                    out[:, :, first - start : last - start] = src[
                        :, q, :, first - q * QUARTER : last - q * QUARTER
                    ]
        outs[-2][...] = src[:, :, :, 1920:2688]
        for place in range(3):
            blocks = [src[block, place, :, 2688:2944].astype(full) for block in (0, 1)]
            for block, row, lane, to_row, to_lane in up_tiles():
                outs[-1][place, to_row : to_row + 8, to_lane : to_lane + 128] = blocks[block][
                    row : row + 8, lane : lane + 128
                ]

    shapes = [(16, 48, width) for _, _, width in WEIGHTS] + [(16, 4, 48, 768)]
    return pl.pallas_call(
        body,
        grid=(8,),
        out_shape=[jax.ShapeDtypeStruct(shape, low) for shape in shapes]
        + [jax.ShapeDtypeStruct((3, WIDE, D), full)],
        in_specs=[pl.BlockSpec((2, 4, 48, 2944), lambda g: (g, 0, 0, 0))],
        out_specs=[
            pl.BlockSpec((2, *shape[1:]), (lambda g: (g, 0, 0)) if len(shape) == 3 else (lambda g: (g, 0, 0, 0)))
            for shape in shapes
        ]
        + [pl.BlockSpec((3, R, D), lambda g: (0, g, 0))],
        compiler_params=pltpu.CompilerParams(vmem_limit_bytes=16 * 2**20),
        name="unpack_weights",
    )(gathered)


def pack_ff(grad_in, grad_out):
    def body(gin, gout, out):
        for q in range(4):
            out[0, q, :48, :] = gin[0, :, 768 * q : 768 * (q + 1)]
            out[0, q, 48:96, :] = gout[0, q]
            out[0, q, 96:, :] = jnp.zeros((FF_ROWS - 96, D), low)

    return pl.pallas_call(
        body,
        grid=(16,),
        out_shape=jax.ShapeDtypeStruct((16, 4, FF_ROWS, D), low),
        in_specs=[
            pl.BlockSpec((1, 48, FF), lambda g: (g, 0, 0)),
            pl.BlockSpec((1, 4, 48, D), lambda g: (g, 0, 0, 0)),
        ],
        out_specs=pl.BlockSpec((1, 4, FF_ROWS, D), lambda g: (g, 0, 0, 0)),
        compiler_params=pltpu.CompilerParams(vmem_limit_bytes=6 * 2**20),
        name="pack_ff",
    )(grad_in.reshape(16, 48, FF), grad_out.reshape(16, 4, 48, D)).reshape(64, FF_ROWS, D)


def pack_gradients(core, lefts, jobs, downs, gain, ups, widths):
    quarter = sum(widths) - 256
    count = len(jobs)
    segments = []
    bounds = [sum(widths[:i]) for i in range(len(widths) + 1)]

    def add(source, source_lane, q, lane, width):
        for part in range(len(widths)):
            first, last = max(lane, bounds[part]), min(lane + width, bounds[part + 1])
            if first < last:
                segments.append((source, source_lane + first - lane, q, part, first - bounds[part], last - first))

    for column in range(count + 1):
        for q in range(4):
            first, last = max(column * D, q * quarter), min(column * D + D, (q + 1) * quarter)
            if first < last:
                add(column, first - column * D, q, first - q * quarter, last - first)
    for q in range(3):
        add(None, 0, q, quarter, 256)
    filled = (count + 1) * D - 3 * quarter
    add("nothing", 0, 3, filled, sum(widths) - filled)
    rows = 384

    def body(core_ref, *rest):
        left_refs, rest = rest[: len(lefts)], rest[len(lefts) :]
        right_refs, rest = rest[:count], rest[count:]
        down_refs, gain_ref, tables, outs, made = rest[:3], rest[3], rest[4:7], rest[7:-1], rest[-1]
        first_down = down_refs[0][...] + gain_ref[...]
        made[count, :, :PLACE] = first_down
        for place in (1, 2):
            made[count, :, place * PLACE : (place + 1) * PLACE] = down_refs[place][...]
        for index, left in enumerate(left_refs):
            turned = left[...].reshape(-1, rows).T
            for job, (of_left, _, _) in enumerate(jobs):
                if of_left == index:
                    right = right_refs[job][...].reshape(-1, D)
                    made[job] = mm(turned, right).astype(low)
        blocks = []
        for place in range(3):
            by_lane = {0: [], 128: []}
            for pair in range(rows // 96):
                tiles = {
                    (block, row, lane): tables[place][R * pair + from_row : R * pair + from_row + 8, from_lane : from_lane + 128]
                    for block, row, lane, from_row, from_lane in up_tiles()
                }
                nothing = jnp.zeros((8, 128), full)
                for lane in (0, 128):
                    by_lane[lane] += [
                        tiles.get((block, 8 * row, lane), nothing) for block in (0, 1) for row in range(6)
                    ]
            blocks.append([jnp.concatenate(by_lane[lane], axis=0).astype(low) for lane in (0, 128)])
        for mine in (0, 1):

            @pl.when(core_ref[0] == mine)
            def _():
                for column, from_lane, q, part, lane, width in segments:
                    out = outs[2 * part + (q % 2 != mine)]
                    lanes = slice(from_lane, from_lane + width)
                    if column is None:
                        for piece in range(width // 128):
                            out[q // 2, :, lane + 128 * piece : lane + 128 * (piece + 1)] = blocks[q][
                                from_lane // 128 + piece
                            ]
                    elif column == "nothing":
                        out[q // 2, :, lane : lane + width] = jnp.zeros((rows, width), low)
                    elif column == 5:
                        out[q // 2, :, lane : lane + width] = made[count, :, lanes]
                    else:
                        out[q // 2, :, lane : lane + width] = made[column - (column > 5), :, lanes]

    shapes = [(2, D, width) for width in widths for _ in range(2)]
    whole = pl.Buffered(1)
    outs = pl.pallas_call(
        body,
        grid=(D // rows,),
        out_shape=[jax.ShapeDtypeStruct(shape, low) for shape in shapes],
        in_specs=[pl.BlockSpec(memory_space=pltpu.SMEM)]
        + [pl.BlockSpec((2, length, rows), partial(lambda block, g: (0, block, g), block)) for _, block, length in lefts]
        + [
            pl.BlockSpec((2, length, D), partial(lambda block, g: (0, block, 0), block), pipeline_mode=whole)
            for (_, right, block), length in zip(jobs, [lefts[of_left][2] for of_left, _, _ in jobs])
        ]
        + [pl.BlockSpec((rows, PLACE), lambda g: (g, 0))] * 4
        + [pl.BlockSpec((R * rows // 96, D), lambda g: (g, 0))] * 3,
        out_specs=[pl.BlockSpec((2, rows, shape[2]), lambda g: (0, g, 0)) for shape in shapes],
        scratch_shapes=[pltpu.VMEM((count + 1, rows, D), low)],
        compiler_params=pltpu.CompilerParams(vmem_limit_bytes=32 * 2**20),
        cost_estimate=pl.CostEstimate(flops=1, bytes_accessed=1, transcendentals=0),
        name="pack_gradients",
    )(core.reshape(1), *[left for left, _, _ in lefts], *[right for _, right, _ in jobs], *downs, gain, *ups)
    return outs[0::2], outs[1::2]


def over_cores(send):
    return [swap(part, "dp", 1) for part in send]


def ring_order(part):
    dp = lax.axis_index("dp")
    y, z = (dp // 4) % 4, dp // 16
    along_y, along_z = (2, y, 2), (1, z, 4)
    return (along_y, along_z) if part % 2 == 0 else (along_z, along_y)


def first_piece(keep, got, part, step):
    axis, position, _ = ring_order(part)[0]
    shape = (2, 4, 4, 48, keep.shape[2])
    mine = lax.dynamic_index_in_dim(keep.reshape(shape), position ^ step, axis, keepdims=False)
    other = lax.dynamic_index_in_dim(got.reshape(shape), position ^ step, axis, keepdims=False)
    return mine.astype(full) + other.astype(full)


def first_exchange(keep, got):
    return [
        [
            swap(first_piece(keep[part], got[part], part, step).astype(low), "dp", step << ring_order(part)[0][2])
            for step in (1, 2, 3)
        ]
        for part in range(len(keep))
    ]


def first_sum(keep, got, received):
    sums = []
    for part in range(len(keep)):
        total = first_piece(keep[part], got[part], part, 0)
        for block in received[part]:
            total = total + block.astype(full)
        sums.append(total.astype(low))
    return sums


def second_piece(half, part, step):
    position = ring_order(part)[1][1]
    return lax.dynamic_index_in_dim(half, position ^ step, 1, keepdims=False)


def second_exchange(halves):
    return [
        [swap(second_piece(half, part, step), "dp", step << ring_order(part)[1][2]) for step in (1, 2, 3)]
        for part, half in enumerate(halves)
    ]


def second_sum(halves, received):
    sums = []
    for part, half in enumerate(halves):
        total = second_piece(half, part, 0).astype(full)
        for block in received[part]:
            total = total + block.astype(full)
        sums.append(total.astype(low))
    return jnp.concatenate(sums, axis=2)


def over_group(both):
    me = lax.axis_index("dp") % 4
    table = both[:, :, 1792:].reshape(2, 12, 1024)

    def rows_of(member):
        return jnp.concatenate([lax.dynamic_slice_in_dim(both, member * 12, 12, 1)[:, :, :1792], table], axis=2)

    halves = []
    for core_step in (0, 1):
        blocks = []
        for x_step in (0, 2):
            step = core_step | x_step
            block = rows_of(me ^ step)
            moved = block if step == 0 else swap(block, "dp", step)
            other = lax.ppermute(
                block, ("dp", "seq"), [(i, i ^ (2 * step + 1)) for i in range(lax.axis_size(("dp", "seq")))]
            )
            blocks.append(moved.astype(full) + other.astype(full))
        halves.append((blocks[0] + blocks[1]).astype(low))
    even = lax.axis_index("dp") % 2 == 0
    first, second = jnp.where(even, halves[0], halves[1]), jnp.where(even, halves[1], halves[0])
    total = jnp.stack([first, second], axis=1).reshape(4, 12, 2816)
    return total[:, :, :1792], total[:, :, 1792:].reshape(4, 48, 256)


STEP = 3
LANES = 128 * STEP


def bias_of(row_docs, column_docs, keys_axis, causal):
    shape = (row_docs.shape[0], column_docs.shape[1])
    allowed = row_docs == column_docs
    if causal:
        key = lax.broadcasted_iota(jnp.int32, shape, keys_axis)
        query = lax.broadcasted_iota(jnp.int32, shape, 1 - keys_axis) + (shape[keys_axis] - shape[1 - keys_axis])
        allowed = allowed & (key <= query)
    return jnp.where(allowed, 0.0, masked_out)


def dot_turned(left, right):
    return lax.dot_general(left, right, (((1,), (1,)), ((), ())), preferred_element_type=full)


def both_heads(pair):
    lane = lax.broadcasted_iota(jnp.int32, pair.shape, 1)
    return jnp.concatenate([jnp.where(lane < HD, pair, 0.0), jnp.where(lane < HD, 0.0, pair)], axis=0).astype(low)


def forward_kernel(causal, q_ref, k_ref, v_ref, qd_ref, kd_ref, out_ref, lse_ref, bias):
    @pl.when(pl.program_id(1) == 0)
    def _():
        bias[...] = bias_of(qd_ref[0], kd_ref[0], 1, causal)

    lane = lax.broadcasted_iota(jnp.int32, (ROWS, 128), 1)
    for pair in range(STEP):
        lanes = slice(pair * 128, (pair + 1) * 128)
        queries = both_heads(q_ref[0, :, lanes].astype(full) * scale)
        allowed = bias[...]
        score = dot_turned(queries, k_ref[0, :, lanes]) + jnp.concatenate([allowed, allowed], axis=0)
        maximum = jnp.max(score, axis=1, keepdims=True)
        exponent = jnp.exp(score - maximum)
        total = jnp.sum(exponent, axis=1, keepdims=True)
        prob = (exponent * (1.0 / total)).astype(low)
        out = mm(prob, v_ref[0, :, lanes])
        logs = maximum + jnp.log(total)
        out_ref[0, :, lanes] = jnp.where(lane < HD, out[:ROWS], out[ROWS:]).astype(low)
        lse_ref[0, pair] = jnp.where(lane < 1, logs[:ROWS], logs[ROWS:]).T[:2]


def backward_kernel(causal, q_ref, k_ref, v_ref, kd_ref, qd_ref, do_ref, lse_ref, dq_ref, dk_ref, dv_ref, bias):
    @pl.when(pl.program_id(1) == 0)
    def _():
        bias[...] = bias_of(kd_ref[0], qd_ref[0], 0, causal)

    for pair in range(STEP):
        lanes = slice(pair * 128, (pair + 1) * 128)
        queries = both_heads(q_ref[0, :, lanes].astype(full) * scale)
        grads = both_heads(do_ref[0, :, lanes].astype(full))
        keys, values = k_ref[0, :, lanes], v_ref[0, :, lanes]
        allowed = bias[...]
        logs = jnp.concatenate([lse_ref[0, pair, :1, :], lse_ref[0, pair, 1:, :]], axis=1)
        score = dot_turned(keys, queries) + jnp.concatenate([allowed, allowed], axis=1)
        prob = jnp.exp(score - logs)
        dprob = dot_turned(values, grads)
        inner = jnp.sum(dprob * prob, axis=0, keepdims=True)
        dscore = (prob * (dprob - inner)).astype(low)
        dq = mm(keys.T, dscore) * scale
        dq_ref[0, :, lanes] = jnp.concatenate([dq[:HD, :ROWS], dq[HD:, ROWS:]], axis=0).T.astype(low)
        dk_ref[0, :, lanes] = mm(dscore, queries).astype(low)
        dv_ref[0, :, lanes] = mm(prob.astype(low), grads).astype(low)


def attention_specs(keys, query_block, key_lane, value_lane):
    return [
        pl.BlockSpec((1, ROWS, LANES), lambda p, h: (p, query_block, h)),
        pl.BlockSpec((1, keys, LANES), lambda p, h: (p, 0, key_lane // STEP + h)),
        pl.BlockSpec((1, keys, LANES), lambda p, h: (p, 0, value_lane // STEP + h)),
    ]


def column_row(columns, rows):
    return [
        pl.BlockSpec((1, columns, 1), lambda p, h: (p, 0, 0)),
        pl.BlockSpec((1, 1, rows), lambda p, h: (p, 0, 0)),
    ]


def attend(queries, keys_values, lanes, key_docs, query_docs, causal):
    packs, keys = keys_values.shape[:2]
    query_block = queries.shape[1] // ROWS - 1
    return pl.pallas_call(
        partial(forward_kernel, causal),
        grid=(packs, PAIRS // STEP),
        in_specs=attention_specs(keys, query_block, *lanes) + column_row(ROWS, keys),
        out_specs=[
            pl.BlockSpec((1, ROWS, LANES), lambda p, h: (p, 0, h)),
            pl.BlockSpec((1, STEP, 2, ROWS), lambda p, h: (p, h, 0, 0)),
        ],
        out_shape=[
            jax.ShapeDtypeStruct((packs, ROWS, D), low),
            jax.ShapeDtypeStruct((packs, PAIRS, 2, ROWS), full),
        ],
        scratch_shapes=[pltpu.VMEM((ROWS, keys), full)],
        compiler_params=pltpu.CompilerParams(vmem_limit_bytes=16 * 2**20),
        cost_estimate=pl.CostEstimate(
            flops=4 * packs * HEADS * ROWS * keys * 256,
            bytes_accessed=2 * packs * D * (2 * ROWS + 2 * keys),
            transcendentals=packs * HEADS * ROWS * keys,
        ),
        name="attend",
    )(queries, keys_values, keys_values, query_docs[:, :, None], key_docs[:, None, :])


def attend_back(queries, keys_values, lanes, key_docs, query_docs, causal, grad_out, lse):
    packs, keys = keys_values.shape[:2]
    query_block = queries.shape[1] // ROWS - 1
    own = pl.BlockSpec((1, ROWS, LANES), lambda p, h: (p, 0, h))
    every = pl.BlockSpec((1, keys, LANES), lambda p, h: (p, 0, h))
    return pl.pallas_call(
        partial(backward_kernel, causal),
        grid=(packs, PAIRS // STEP),
        in_specs=attention_specs(keys, query_block, *lanes)
        + column_row(keys, ROWS)
        + [own, pl.BlockSpec((1, STEP, 2, ROWS), lambda p, h: (p, h, 0, 0))],
        out_specs=[own, every, every],
        out_shape=[
            jax.ShapeDtypeStruct((packs, ROWS, D), low),
            jax.ShapeDtypeStruct((packs, keys, D), low),
            jax.ShapeDtypeStruct((packs, keys, D), low),
        ],
        scratch_shapes=[pltpu.VMEM((keys, ROWS), full)],
        compiler_params=pltpu.CompilerParams(vmem_limit_bytes=16 * 2**20),
        cost_estimate=pl.CostEstimate(flops=1, bytes_accessed=1, transcendentals=0),
        name="attend_back",
    )(queries, keys_values, keys_values, key_docs[:, :, None], query_docs[:, None, :], grad_out, lse)


def norm_apply(resid, gains):
    inverse = lax.rsqrt(jnp.mean(resid * resid, axis=-1, keepdims=True) + epsilon)
    return resid * inverse * gains[:, None, :]


def norm_back(resid, gains, grad_norm):
    inverse = lax.rsqrt(jnp.mean(resid * resid, axis=-1, keepdims=True) + epsilon)
    unit = resid * inverse
    grad_gain = jnp.sum(grad_norm * unit, axis=1)
    scaled = grad_norm * gains[:, None, :]
    grad = inverse * (scaled - unit * jnp.mean(scaled * unit, axis=-1, keepdims=True))
    return grad, grad_gain


def gelu_back(pre_act, grad_act):
    _, pull_back = jax.vjp(jax.nn.gelu, pre_act)
    return pull_back(grad_act)[0]


def project(left, weight):
    return jnp.einsum("prd,de->pre", left, weight, preferred_element_type=full)


def project_back(grad_out, weight):
    return jnp.einsum("pre,de->prd", grad_out, weight, preferred_element_type=full)


def weight_grad(left, grad_out):
    return jnp.einsum("prd,pre->de", left, grad_out, preferred_element_type=full)


def adapter_forward(branch, down_gen, up_gen, task_mask):
    branch_low = branch.astype(low)
    pre_act = project(branch_low, down_gen)
    hidden = jnp.where(task_mask, jax.nn.gelu(pre_act), 0.0).astype(low)
    return project(hidden, up_gen), (branch_low, pre_act, hidden)


def adapter_backward(grad_resid, kept, down_gen, up_gen, task_mask):
    branch_low, pre_act, hidden = kept
    grad_adapt = grad_resid.astype(low)
    grad_up = jnp.einsum("prk,prd->pkd", hidden, grad_adapt, preferred_element_type=full)
    grad_hidden = project_back(grad_adapt, up_gen)
    grad_pre = jnp.where(task_mask, gelu_back(pre_act, grad_hidden), 0.0).astype(low)
    grad_down = jnp.einsum("prd,prk->pdk", branch_low, grad_pre, preferred_element_type=full)
    grad_branch = grad_resid + project_back(grad_pre, down_gen)
    return lax.optimization_barrier(
        (
            grad_branch.astype(low),
            jnp.sum(grad_down.astype(low).astype(full), axis=0).astype(low),
            jnp.sum(grad_up.astype(low).astype(full), axis=0)[:WIDE],
        )
    )


def code_table(task_table, place_table, proj_in, proj_out):
    shape = (3, NTASK, TE)
    joined = jnp.concatenate(
        [jnp.broadcast_to(task_table[None], shape), jnp.broadcast_to(place_table[:, None], shape)], axis=-1
    ).reshape(3 * NTASK, 2 * TE)
    hidden = jax.nn.gelu(jnp.dot(joined, proj_in, precision=highest_precision))
    return jnp.dot(hidden, proj_out, precision=highest_precision)


def generate(task_table, place_table, proj_in, proj_out, gen_down, gen_up):
    def body(task, place, first, second, down, up, codes_ref, down_ref, up_ref):
        joined = jnp.concatenate(
            [jnp.concatenate([task[...]] * 3, axis=0)]
            + [jnp.concatenate([jnp.broadcast_to(place[a : a + 1], (NTASK, TE)) for a in range(3)], axis=0)],
            axis=1,
        )
        hidden = jax.nn.gelu(jnp.dot(joined, first[...], precision=highest_precision))
        codes = jnp.dot(hidden, second[...], precision=highest_precision).astype(low)
        codes_ref[...] = codes
        down_ref[...] = mm(codes, down[...]).astype(low)
        up_ref[...] = mm(codes, up[...]).astype(low)

    count = 3 * NTASK
    return pl.pallas_call(
        body,
        out_shape=[jax.ShapeDtypeStruct((count, width), low) for width in (TE, 288, 288)],
        name="generate",
    )(task_table, place_table, proj_in, proj_out, gen_down, gen_up)


def up_to_block(rows):
    lead = rows.shape[:-2]
    tiles = jnp.moveaxis(rows.reshape(*lead, 8, 9, 128), -2, -3).reshape(*lead, 72, 128)
    tiles = jnp.pad(tiles, [(0, 0)] * len(lead) + [(0, 24), (0, 0)]).reshape(*lead, 2, 48, 128)
    return jnp.moveaxis(tiles, -3, -2).reshape(*lead, 48, 256)


def up_from_block(block):
    lead = block.shape[:-2]
    tiles = jnp.moveaxis(block.reshape(*lead, 48, 2, 128), -2, -3).reshape(*lead, 96, 128)[..., :72, :]
    return jnp.moveaxis(tiles.reshape(*lead, 9, 8, 128), -3, -2).reshape(*lead, 8, 1152)


def over_dp(value):
    for shift in (0, 2, 4):
        first = value + swap(value, "dp", 1 << shift)
        second = swap(value, "dp", 2 << shift) + swap(value, "dp", 3 << shift)
        value = first + second
    return value


def both_halves(part):
    return part.astype(full) + swap(part, "seq", 1).astype(full)


def shards(
    inputs,
    memory,
    cotangent,
    seg_ids,
    mem_seg,
    tasks,
    self_qkv,
    self_out,
    cross_query,
    cross_kv,
    cross_out,
    ff_in,
    ff_out,
    gen_down,
    gen_up,
    gen_gain,
    task_table,
    place_table,
    proj_in,
    proj_out,
):
    seq_index = lax.axis_index("seq")
    core = lax.axis_index("dp") % 2
    packs, row_count = inputs.shape[:2]
    mem_count = memory.shape[1]

    _, hyper_pull = jax.vjp(code_table, task_table, place_table, proj_in, proj_out)
    codes_low, own_down, own_up = generate(task_table, place_table, proj_in, proj_out, gen_down, gen_up)
    own_down = own_down.reshape(3, NTASK, 12, R)
    own_down = own_down.transpose(2, 0, 3, 1).reshape(12, 3, WIDE)
    spare = jnp.pad(gen_gain.T[:, None, :], ((0, 0), (0, 2), (0, 0)))
    own_down = jnp.concatenate([own_down, spare], axis=2).reshape(12, 3 * PLACE)
    up_pieces = jnp.pad(own_up.reshape(3, 12, 192), ((0, 1), (0, 0), (0, 64)))
    early = jnp.concatenate([self_qkv, own_down[:, :PLACE]], axis=1).reshape(12, 4, EARLY)
    late = [self_out, cross_query, cross_out, cross_kv, own_down[:, PLACE:], jnp.zeros((12, 256), low), ff_in]
    late = jnp.concatenate(late, axis=1).reshape(12, 4, QUARTER)
    exchanged = group_exchange(
        jnp.concatenate([jnp.concatenate([early, late], axis=2).transpose(1, 0, 2), up_pieces], axis=2)
    )
    early = exchanged[:, :, :EARLY].reshape(48, EARLY)
    late = exchanged[:, :, EARLY:2560].reshape(48, QUARTER)
    up_rows = exchanged[:, :, 2560:2752].reshape(4, NTASK, 288).transpose(1, 0, 2).reshape(NTASK, 1152)
    block = jnp.concatenate([late, ff_out, up_to_block(up_rows)], axis=1)

    gathered = lax.all_gather(block, "dp", axis=0, tiled=False)
    ids = jnp.concatenate([seg_ids, mem_seg], axis=1)
    early, other_ids, other_memory, earlier = lax.optimization_barrier(
        (
            early_gather(early),
            swap(ids, "seq", 1),
            swap(memory, "seq", 1),
            lax.ppermute(inputs, "seq", [(0, 1)]),
        )
    )
    mem_rows = jnp.concatenate([memory, other_memory], axis=1)
    mem_docs = jnp.concatenate([mem_seg, other_ids[:, row_count:]], axis=1)
    earlier_docs = jnp.where(seq_index > 0, other_ids[:, :row_count], -1)
    key_docs = jnp.concatenate([earlier_docs, seg_ids], axis=1)
    query_docs = seg_ids

    early = unpack_early(early, swap(early, "dp", 1))
    full_self_qkv, down_zero = [piece.reshape(D, piece.shape[2]) for piece in early]
    pieces = unpack(gathered.reshape(16, 4, 48, 2944))
    full_self_out, full_query, full_cross_out, full_mem_kv, full_down, full_ff_in = [
        piece.reshape(D, piece.shape[2]) for piece in pieces[:6]
    ]
    full_ff_out = pieces[6].reshape(FF, D)
    full_up = jnp.pad(pieces[7].astype(low), ((0, 0), (0, PLACE - WIDE), (0, 0)))
    full_gain = down_zero[:, WIDE:]
    down_of = [down_zero, full_down[:, :PLACE], full_down[:, PLACE:]]
    up_of = [full_up[a] for a in range(3)]

    gain_table = 1.0 + jnp.einsum("xt,ct->xc", codes_low, full_gain, preferred_element_type=full)
    onehot = (tasks[:, None] == jnp.arange(NTASK, dtype=jnp.int32)[None, :]).astype(full)
    gain_all = jnp.einsum(
        "pt,atc->pac", onehot, gain_table.reshape(3, NTASK, D), precision=highest_precision
    )
    column = jnp.arange(PLACE, dtype=jnp.int32)
    task_mask = ((tasks[:, None] == (column % NTASK)[None, :]) & (column < WIDE)[None, :])[:, None, :]

    both_rows = jnp.concatenate([earlier, inputs], axis=1).astype(full)
    resid_zero = both_rows[:, row_count:]
    normed_one = norm_apply(both_rows, gain_all[:, 0]).astype(low)
    self_proj = project(normed_one, full_self_qkv).astype(low)
    mem_kv = project(mem_rows, full_mem_kv).astype(low)
    attended_one, total_one = attend(self_proj, self_proj, (6, 12), key_docs, query_docs, True)
    branch_one = project(attended_one, full_self_out)
    adapt_one, kept_one = adapter_forward(branch_one, down_of[0], up_of[0], task_mask)
    resid_one = resid_zero + branch_one + adapt_one
    normed_two = norm_apply(resid_one, gain_all[:, 1]).astype(low)
    cross_queries = project(normed_two, full_query).astype(low)
    attended_two, total_two = attend(cross_queries, mem_kv, (0, 6), mem_docs, query_docs, False)
    branch_two = project(attended_two, full_cross_out)
    adapt_two, kept_two = adapter_forward(branch_two, down_of[1], up_of[1], task_mask)
    resid_two = resid_one + branch_two + adapt_two
    normed_three = norm_apply(resid_two, gain_all[:, 2]).astype(low)
    ff_pre = project(normed_three, full_ff_in)
    ff_hidden = jax.nn.gelu(ff_pre).astype(low)
    branch_three = project(ff_hidden, full_ff_out)
    adapt_three, kept_three = adapter_forward(branch_three, down_of[2], up_of[2], task_mask)
    mixed = (resid_two + branch_three + adapt_three).astype(low)

    grad_three = cotangent.astype(full)
    branch_grad, down_three, up_three = adapter_backward(grad_three, kept_three, down_of[2], up_of[2], task_mask)
    grad_ff_out = weight_grad(ff_hidden, branch_grad).astype(low)
    hidden_grad = project_back(branch_grad, full_ff_out)
    pre_grad = gelu_back(ff_pre, hidden_grad).astype(low)
    grad_ff_in = weight_grad(normed_three, pre_grad).astype(low)
    resid_grad, gain_three = norm_back(resid_two, gain_all[:, 2], project_back(pre_grad, full_ff_in))
    grad_two = grad_three + resid_grad
    ff_blocks, grad_two = lax.optimization_barrier((pack_ff(grad_ff_in, grad_ff_out), grad_two))
    part_ff = lax.psum_scatter(ff_blocks, "dp", scatter_dimension=0, tiled=False)[:96]

    branch_grad, down_two, up_two = adapter_backward(grad_two, kept_two, down_of[1], up_of[1], task_mask)
    grad_two_low = branch_grad
    out_grad = project_back(branch_grad, full_cross_out).astype(low)
    query_two, key_two, value_two = attend_back(
        cross_queries, mem_kv, (0, 6), mem_docs, query_docs, False, out_grad, total_two
    )
    rows_grad = project_back(key_two, full_mem_kv[:, :D]) + project_back(value_two, full_mem_kv[:, D:])
    grad_memory = rows_grad[:, :mem_count] + swap(rows_grad[:, mem_count:].astype(low), "seq", 1).astype(full)
    resid_grad, gain_two = norm_back(resid_one, gain_all[:, 1], project_back(query_two, full_query))
    grad_one = grad_two + resid_grad

    branch_grad, down_one, up_one = adapter_backward(grad_one, kept_one, down_of[0], up_of[0], task_mask)
    grad_one_low = branch_grad
    gain_sum = jnp.einsum("pt,pac->atc", onehot, jnp.stack([gain_two, gain_three], 1), precision=highest_precision)
    gain_sum = gain_sum.reshape(2 * NTASK, D)
    codes_full = codes_low.astype(full)
    spare_codes = jnp.pad(codes_full[NTASK:], ((0, 0), (WIDE, 0)))
    grad_gain = jnp.einsum("xc,xt->ct", gain_sum, spare_codes, precision=highest_precision).astype(low)
    out_grad = project_back(branch_grad, full_self_out).astype(low)
    query_grad, key_grad, value_grad = attend_back(
        self_proj, self_proj, (6, 12), key_docs, query_docs, True, out_grad, total_one
    )
    norm_grad = project_back(key_grad, full_self_qkv[:, D : 2 * D]) + project_back(
        value_grad, full_self_qkv[:, 2 * D :]
    )
    returned = lax.ppermute(norm_grad[:, :row_count].astype(low), "seq", [(1, 0)])
    keep, send = pack_gradients(
        core,
        [
            (attended_one, 0, ROWS),
            (normed_two, 0, ROWS),
            (attended_two, 0, ROWS),
            (mem_rows, 0, 2 * mem_count),
            (normed_one, 1, ROWS),
            (normed_one, 0, 2 * ROWS),
        ],
        [
            (0, grad_one_low, 0),
            (1, query_two, 0),
            (2, grad_two_low, 0),
            (3, key_two, 0),
            (3, value_two, 0),
            (4, query_grad, 0),
            (5, key_grad, 0),
            (5, value_grad, 0),
        ],
        (down_one, down_two, down_three),
        grad_gain,
        (up_one, up_two, up_three),
        (1024, 1024),
    )
    got = over_cores(send)
    received = first_exchange(keep, got)
    norm_grad = norm_grad[:, row_count:] + project_back(query_grad, full_self_qkv[:, :D]) + returned.astype(full)
    resid_grad, gain_one = norm_back(resid_zero, gain_all[:, 0], norm_grad)
    grad_input = grad_one + resid_grad
    gain_first = jnp.einsum("pt,pc->tc", onehot, gain_one, precision=highest_precision)
    gain_codes = jnp.einsum("xc,ct->xt", gain_sum, full_gain.astype(full), precision=highest_precision)
    gain_part = jnp.concatenate(
        [gain_first.reshape(3 * NTASK, 256), jnp.pad(gain_codes, ((NTASK, 0), (0, 0)))], axis=1
    )
    gain_part = gain_part + swap(gain_part, "seq", 1)
    halves = first_sum(keep, got, received)
    both = second_sum(halves, second_exchange(halves))
    pieces, up_blocks = over_group(both)
    rest = pieces.transpose(1, 0, 2).reshape(12, 7168).astype(full)
    up_rows = up_from_block(up_blocks[:3]).reshape(3 * NTASK, 1152)
    up_table = lax.dynamic_slice_in_dim(up_rows, (lax.axis_index("dp") % 4) * 288, 288, 1).astype(full)
    sum_self_out = rest[:, :768]
    sum_query = rest[:, 768:1536]
    sum_cross_out = rest[:, 1536:2304]
    sum_mem_kv = rest[:, 2304:3840]
    down_table = rest[:, 3840:4608].reshape(12, 3, PLACE)[:, :, :WIDE].reshape(12, 3, R, NTASK)
    down_table = down_table.transpose(1, 3, 0, 2).reshape(3 * NTASK, 288)
    sum_qkv = rest[:, 4608:6912]
    sum_down = jnp.einsum("xt,xc->tc", codes_full, down_table, precision=highest_precision)
    sum_up = jnp.einsum("xt,xc->tc", codes_full, up_table, precision=highest_precision)

    grad_codes = jnp.einsum("xc,tc->xt", down_table, gen_down.astype(full), precision=highest_precision) + jnp.einsum(
        "xc,tc->xt", up_table, gen_up.astype(full), precision=highest_precision
    )
    joint = gain_part + jnp.pad(grad_codes, ((0, 0), (256, 0)))
    joint, part_ff = lax.optimization_barrier((over_dp(joint), part_ff))
    part_ff = both_halves(part_ff)
    sum_ff_in = from_quarters(part_ff[:48].astype(low)).astype(full)
    sum_ff_out = part_ff[48:]
    gain_first = joint[:, :256].reshape(NTASK, D)
    first_codes = jnp.einsum("xc,ct->xt", gain_first, full_gain.astype(full), precision=highest_precision)
    grad_codes = joint[:, 256:] + jnp.pad(first_codes, ((0, 2 * NTASK), (0, 0)))
    table_sum, place_sum, proj_in_sum, proj_out_sum = hyper_pull(grad_codes)
    own_gains = lax.dynamic_slice_in_dim(gain_first, lax.axis_index("dp") * 12, 12, 1)
    sum_gain = jnp.einsum("xt,xc->tc", codes_full[:NTASK], own_gains, precision=highest_precision)
    sum_gain = sum_gain + rest[:, 3840 + WIDE : 3840 + PLACE].T
    return (
        mixed,
        grad_input,
        grad_memory,
        sum_qkv,
        sum_self_out,
        sum_query,
        sum_mem_kv,
        sum_cross_out,
        sum_ff_in,
        sum_ff_out,
        sum_down,
        sum_up,
        sum_gain,
        table_sum,
        place_sum,
        proj_in_sum,
        proj_out_sum,
    )


def solution(mesh):
    in_specs = (
        P("dp", "seq", None),
        P("dp", "seq", None),
        P("dp", "seq", None),
        P("dp", "seq"),
        P("dp", "seq"),
        P("dp"),
        P("dp", None),
        P("dp", None),
        P("dp", None),
        P("dp", None),
        P("dp", None),
        P("dp", None),
        P("dp", None),
        P(None, "dp"),
        P(None, "dp"),
        P(None, "dp"),
        P(),
        P(),
        P(),
        P(),
    )
    out_specs = (
        P("dp", "seq", None),
        P("dp", "seq", None),
        P("dp", "seq", None),
        P("dp", None),
        P("dp", None),
        P("dp", None),
        P("dp", None),
        P("dp", None),
        P("dp", None),
        P("dp", None),
        P(None, "dp"),
        P(None, "dp"),
        P(None, "dp"),
        P(),
        P(),
        P(),
        P(),
    )
    return jax.shard_map(shards, mesh=mesh, in_specs=in_specs, out_specs=out_specs, check_vma=False)
```

time: 2200 us -> 447 us (0.20)
  blocking collectives: 963 us -> 0 us
  waiting for transfers between devices: 503 us -> 157 us
  local copies, waits for them, and re-layouts: 243 us -> 47.6 us
  starting transfers between devices: 248 us -> 66.9 us
  matrix products: 164 us -> 62.9 us
  Pallas kernels: 0 us -> 57.3 us
    unnamed x2 -> x0, blocking collectives: 744 us -> none
    all_gather x9 -> x1, waiting for transfers between devices: 350 us -> 38 us  [shards(): gathered = lax.all_gather(block, 'dp', axis=0, tiled=False)]
    unnamed x99 -> x0, starting transfers between devices: 242 us -> none
    all_gather x4 -> x0, blocking collectives: 148 us -> none  [the longest x1 102 us: shards(): lax.all_gather(gen_gain, 'dp', axis=1, tiled=True)]
    psum x3 -> x0, waiting for transfers between devices: 126 us -> none  [the longest x1 126 us: shards(): lax.psum((table_grad, place_grad, proj_in_grad, proj_out_grad), ('dp', 's...]
    unnamed x311 -> x235, local copies, waits for them, and re-layouts: 147 us -> 29.6 us
    dot_general x84 -> x54, matrix products: 164 us -> 62.9 us  [the longest x16 25.1 us: project_back(): jnp.einsum('pre,de->prd', grad_out, weight, preferred_element_type=full)]
    ppermute x2 -> x51, waiting for transfers between devices: 20.9 us -> 119 us  [the longest x45 93.2 us: swap(): return lax.ppermute(value, axis, [(i, i ^ mask) for i in range(count)])]
  transfers between devices with their start and end apart: 114 -> 53, of which waited for: 10 -> 26; matrix products, arithmetic and copies ran while one was open for 35% -> 14% of each run, Pallas kernels for 0% -> 11%
where the time goes in v1:
time: 447 us; the launch traced here: 441 us
  waiting for transfers between devices  157 us (35%)
  starting transfers between devices  66.9 us (15%)
  matrix products  62.9 us (14%)
  Pallas kernels  57.3 us (13%)
  local copies, waits for them, and re-layouts  47.6 us (11%)
  other arithmetic  32.1 us (7%)
  between operations  16.9 us (4%)
    ppermute x45, waiting for transfers between devices, swap(): return lax.ppermute(value, axis, [(i, i ^ mask) for i in range(count)])  93.2 us
    ppermute x45, starting transfers between devices, swap(): return lax.ppermute(value, axis, [(i, i ^ mask) for i in range(count)])  55 us
    all_gather x1, waiting for transfers between devices, shards(): gathered = lax.all_gather(block, 'dp', axis=0, tiled=False)  38 us
    unnamed x235, local copies, waits for them, and re-layouts  29.6 us
    dot_general x16, matrix products, project_back(): jnp.einsum('pre,de->prd', grad_out, weight, preferred_element_type=full)  25.1 us
    pallas_call x2, Pallas kernels, attend_back(): pl.pallas_call(partial(backward_kernel, causal), grid=(packs, PAIRS // ST...  20.9 us
    dot_general x13, matrix products, project(): return jnp.einsum('prd,de->pre', left, weight, preferred_element_type=full)  17.9 us
    ppermute x1, waiting for transfers between devices, shards(): lax.ppermute(norm_grad[:, :row_count].astype(low), 'seq', [(1, 0)])  15.6 us
  transfers between devices with their start and end apart: 53, of which 26 were waited for; matrix products, arithmetic and copies ran while one was open for 14% of the time, Pallas kernels for 11%

profile of v1, /device:TPU:1, one launch (start us, length us, event | category | flops | bytes accessed | tf_op | source)
XLA Modules:
  0.0 441.1 jit_solution(3591288985540526148)
XLA Ops:
  15.2 4.2 collective-permute-start.2
  32.0 3.7 collective-permute-start.5
  46.9 8.5 %collective-permute-done.8 = bf16[4,2,48,640]{3,2,1,0:T(8,128)(2,1)S(1)} collective-permute-done((bf16[4,2,48,640]{3,2,1,0:T(8,128)(2,1)S(1)}, bf16[4,2,48,640]{3,2,1,0:T(8,128)(2,1)S(1)}, u32[]{:S(2)}, u32[]{:S(2)}) %collective-permute-start.8) | collective-permute-done | bytes 491552 | tf_op jit(solution)/shard_map/ppermute | solution.py:37
  57.1 10.3 %collective-permute-done.7 = bf16[4,2,48,640]{3,2,1,0:T(8,128)(2,1)S(1)} collective-permute-done((bf16[4,2,48,640]{3,2,1,0:T(8,128)(2,1)S(1)}, bf16[4,2,48,640]{3,2,1,0:T(8,128)(2,1)S(1)}, u32[]{:S(2)}, u32[]{:S(2)}) %collective-permute-start.7) | collective-permute-done | bytes 491552 | tf_op jit(solution)/shard_map/ppermute | solution.py:37
  84.1 8.4 %unpack_early.1 = (bf16[16,48,2304]{2,1,0:T(8,128)(2,1)S(1)}, bf16[16,48,256]{2,1,0:T(8,128)(2,1)S(1)}) custom-call(s32[3]{0:T(128)S(1)} %pad_add_fusion.9.place_ref, bf16[4,4,2,48,640]{4,3,2,1,0:T(8,128)(2,1)S(1)} %pad_maximum_fusion.own_ref, bf16[4,4,2,48,640]{4,3,2,1,0:T(8,128)(2,1)} %collective-permute-done.13.other_ref), custom_call_target="tpu_custom_call" | custom-call | tf_op jit(solution)/shard_map/unpack_early/pallas_call | solution.py:94
  95.9 4.1 convolution_convert_fusion.q_ref.k_ref.v_ref
  100.0 7.7 %attend.2 = (bf16[2,256,768]{2,1,0:T(8,128)(2,1)S(1)}, f32[2,6,2,256]{3,2,1,0:T(2,128)S(1)}) custom-call(bf16[2,512,2304]{2,1,0:T(8,128)(2,1)S(1)} %convolution_convert_fusion.q_ref.k_ref.v_ref, bf16[2,512,2304]{2,1,0:T(8,128)(2,1)S(1)} %convolution_convert_fusion.q_ref.k_ref.v_ref, bf16[2,512,2304]{2,1,0:T(8,128)(2,1)S(1)} %convolution_convert_fusion.q_ref.k_ref.v_ref, ...), custom_call_target="tpu_custom_call" | custom-call | flops 3221225472 | bytes 4718592 | tf_op jit(solution)/shard_map/attend/pallas_call | solution.py:439
  109.8 38.0 %all-gather.3.cloned.1.call-done = bf16[3072,2944]{1,0:T(8,128)(2,1)} async-done(((bf16[48,2944]{1,0:T(8,128)(2,1)}), bf16[3072,2944]{1,0:T(8,128)(2,1)}) %all-gather.3.cloned.1.call-update) | async-done | bytes 18087952 | tf_op jit(solution)/shard_map/all_gather | solution.py:641
  147.8 6.1 %copy-done.2 = bf16[3072,2944]{1,0:T(8,128)(2,1)S(1)} copy-done((bf16[3072,2944]{1,0:T(8,128)(2,1)S(1)}, bf16[3072,2944]{1,0:T(8,128)(2,1)}, u32[]{:S(2)}) %copy-start.2) | copy-done | bytes 18087960
  163.9 5.4 %attend.3 = (bf16[2,256,768]{2,1,0:T(8,128)(2,1)S(1)}, f32[2,6,2,256]{3,2,1,0:T(2,128)S(1)}) custom-call(bf16[2,256,768]{2,1,0:T(8,128)(2,1)S(1)} %convolution_convert_fusion.4.q_ref, bf16[2,256,1536]{2,1,0:T(8,128)(2,1)S(1)} %convolution_convert_fusion.1.k_ref.v_ref, bf16[2,256,1536]{2,1,0:T(8,128)(2,1)S(1)} %convolution_convert_fusion.1.k_ref.v_ref, ...), custom_call_target="tpu_custom_call" | custom-call | flops 1610612736 | bytes 3145728 | tf_op jit(solution)/shard_map/attend/pallas_call | solution.py:439
  174.3 3.7 fusion.152
  183.6 6.1 %fusion.6 = bf16[2,256,3072]{2,1,0:T(8,128)(2,1)S(1)} fusion(f32[2,256,3072]{2,1,0:T(8,128)S(1)} %fusion.81, bf16[2,256,768]{2,1,0:T(8,128)(2,1)S(1)} %fusion.7, bf16[3072,768,1]{1,0,2:T(8,128)(2,1)S(1)} %bitcast.343), kind=kOutput, calls=%fused_computation.12 | convolution fusion | flops 2447376384 | bytes 14942208 | tf_op jit(solution)/shard_map/pre,de->prd/dot_general | solution.py:510
  189.7 3.8 bitcast_convert_fusion
  202.6 4.6 %copy-done.1 = bf16[16,4,128,768]{3,2,1,0:T(8,128)(2,1)} copy-done((bf16[16,4,128,768]{3,2,1,0:T(8,128)(2,1)}, bf16[16,4,128,768]{3,2,1,0:T(8,128)(2,1)S(1)}, u32[]{:S(2)}) %copy-start.1) | copy-done | bytes 12582936
  217.1 8.3 %attend_back.2 = (bf16[2,256,768]{2,1,0:T(8,128)(2,1)S(1)}, bf16[2,256,768]{2,1,0:T(8,128)(2,1)S(1)}, bf16[2,256,768]{2,1,0:T(8,128)(2,1)S(1)}) custom-call(bf16[2,256,768]{2,1,0:T(8,128)(2,1)S(1)} %copy-done.23, bf16[2,256,1536]{2,1,0:T(8,128)(2,1)S(1)} %convolution_convert_fusion.1.k_ref.v_ref, ...), custom_call_target="tpu_custom_call" | custom-call | flops 1 | bytes 1 | tf_op jit(solution)/shard_map/attend_back/pallas_call | solution.py:467
  233.2 12.6 %attend_back.3 = (bf16[2,256,768]{2,1,0:T(8,128)(2,1)S(1)}, bf16[2,512,768]{2,1,0:T(8,128)(2,1)S(1)}, bf16[2,512,768]{2,1,0:T(8,128)(2,1)S(1)}) custom-call(bf16[2,512,2304]{2,1,0:T(8,128)(2,1)S(1)} %bitcast.318, bf16[2,512,2304]{2,1,0:T(8,128)(2,1)S(1)} %bitcast.318, bf16[2,512,2304]{2,1,0:T(8,128)(2,1)S(1)} %bitcast.318, s32[2,512,1]{2,1,0:T(8,128)S(1)} %copy-done.9, ...), custom_call_target="tpu_custom_call" | custom-call | flops 1 | bytes 1 | tf_op jit(solution)/shard_map/attend_back/pallas_call | solution.py:467
  246.7 10.5 %pack_gradients.1 = (bf16[2,768,1024]{2,1,0:T(8,128)(2,1)S(1)}, bf16[2,768,1024]{2,1,0:T(8,128)(2,1)S(1)}, bf16[2,768,1024]{2,1,0:T(8,128)(2,1)}, bf16[2,768,1024]{2,1,0:T(8,128)(2,1)}) custom-call(s32[1]{0:T(128)} %bitcast.80.core_ref, bf16[2,256,768]{2,1,0:T(8,128)(2,1)S(1)} %copy-done.19, bf16[2,256,768]{2,1,0:T(8,128)(2,1)S(1)} %copy-done.4, ...), custom_call_target="tpu_custom_call" | custom-call | flops 1 | bytes 1 | tf_op jit(solution)/shard_map/pack_gradients/pallas_call | solution.py:247
  271.4 15.6 %collective-permute-done.14 = bf16[2,256,768]{2,1,0:T(8,128)(2,1)S(1)} collective-permute-done((bf16[2,256,768]{2,1,0:T(8,128)(2,1)S(1)}, bf16[2,256,768]{2,1,0:T(8,128)(2,1)S(1)}, u32[]{:S(2)}, u32[]{:S(2)}) %collective-permute-start.14) | collective-permute-done | bytes 786464 | tf_op jit(solution)/shard_map/ppermute | solution.py:735
  302.3 12.4 %collective-permute-done.25 = bf16[2,4,48,1024]{3,0,2,1:T(2,128)(2,1)S(1)} collective-permute-done((bf16[2,4,48,1024]{3,0,2,1:T(2,128)(2,1)S(1)}, bf16[2,4,48,1024]{3,0,2,1:T(2,128)(2,1)S(1)}, u32[]{:S(2)}, u32[]{:S(2)}) %collective-permute-start.25) | collective-permute-done | bytes 786464 | tf_op jit(solution)/shard_map/ppermute | solution.py:37
  314.7 31.4 %collective-permute-done.24 = bf16[2,4,48,1024]{3,0,2,1:T(2,128)(2,1)S(1)} collective-permute-done((bf16[2,4,48,1024]{3,0,2,1:T(2,128)(2,1)S(1)}, bf16[2,4,48,1024]{3,0,2,1:T(2,128)(2,1)S(1)}, u32[]{:S(2)}, u32[]{:S(2)}) %collective-permute-start.24) | collective-permute-done | bytes 786464 | tf_op jit(solution)/shard_map/ppermute | solution.py:37
  363.1 4.3 collective-permute-done.21
  368.7 4.4 %collective-permute-start.34 = (bf16[2,12,2816]{2,0,1:T(2,128)(2,1)S(1)}, bf16[2,12,2816]{2,0,1:T(2,128)(2,1)S(1)}, u32[]{:S(2)}, u32[]{:S(2)}) collective-permute-start(bf16[2,12,2816]{2,0,1:T(2,128)(2,1)S(1)} %get-tuple-element.157), channel_id=1, source_target_pairs={{0,3},{1,2},{2,1},{3,0},{4,7},{5,6},{6,5},{7,4},{8,11},{9,10},{10,... | collective-permute-start | bytes 405512 | tf_op jit(solution)/shard_map/ppermute | solution.py:343
  385.4 6.0 %collective-permute-done.36 = bf16[2,12,2816]{2,0,1:T(2,128)(2,1)S(1)} collective-permute-done((bf16[2,12,2816]{2,0,1:T(2,128)(2,1)S(1)}, bf16[2,12,2816]{2,0,1:T(2,128)(2,1)S(1)}, u32[]{:S(2)}, u32[]{:S(2)}) %collective-permute-start.36) | collective-permute-done | bytes 135200 | tf_op jit(solution)/shard_map/ppermute | solution.py:343
  420.4 7.6 %collective-permute-start.50 = (bf16[12,768]{1,0:T(8,128)(2,1)S(1)}, bf16[12,768]{1,0:T(8,128)(2,1)S(1)}, u32[]{:S(2)}, u32[]{:S(2)}) collective-permute-start(bf16[12,768]{1,0:T(8,128)(2,1)S(1)} %get-tuple-element.154), channel_id=1, source_target_pairs={{0,6},{2,4},{4,2},{6,0},{8,14},{10,12},{12,10},{14,8},{16,22},{18,... | collective-permute-start | bytes 55304 | tf_op jit(solution)/shard_map/ppermute | solution.py:37
  (521 shorter events, 196.7 us)
Async XLA Ops:
  7.2 140.6 %all-gather.3.cloned.1.call-start = ((), (), s32[]{:S(2)}) async-start(), calls=%async_computation.2 | async-start | bytes 18370560 | tf_op jit(solution)/shard_map/all_gather | solution.py:641
  27.2 385.8 %reduce-scatter.2.cloned.1.call-start = ((), (), s32[]{:S(2)}) async-start(), calls=%async_computation.1 | async-start | bytes 12779520 | tf_op jit(solution)/shard_map/reduce_scatter | solution.py:708
  36.4 36.0 %collective-permute-start.12 = (bf16[2,256,768]{2,1,0:T(8,128)(2,1)}, bf16[2,256,768]{2,1,0:T(8,128)(2,1)}, u32[]{:S(2)}, u32[]{:S(2)}) collective-permute-start(bf16[2,256,768]{2,1,0:T(8,128)(2,1)} %param.20), channel_id=1, source_target_pairs={{0,1},{2,3},{4,5},{6,7},{8,9},{10,11},{12,13},{14,15},{16,17},{18,... | collective-permute-start | bytes 2359304 | tf_op jit(solution)/shard_map/ppermute | solution.py:648
  42.8 12.7 %collective-permute-start.8 = (bf16[4,2,48,640]{3,2,1,0:T(8,128)(2,1)S(1)}, bf16[4,2,48,640]{3,2,1,0:T(8,128)(2,1)S(1)}, u32[]{:S(2)}, u32[]{:S(2)}) collective-permute-start(bf16[4,2,48,640]{3,2,1,0:T(8,128)(2,1)S(1)} %get-tuple-element.139), channel_id=1, source_target_pairs={{0,16},{2,18},{4,20},{6,22},{8,24},{10,26},{12,28},{14,30},{16,0},... | collective-permute-start | bytes 1474568 | tf_op jit(solution)/shard_map/ppermute | solution.py:37
  45.7 21.8 %collective-permute-start.7 = (bf16[4,2,48,640]{3,2,1,0:T(8,128)(2,1)S(1)}, bf16[4,2,48,640]{3,2,1,0:T(8,128)(2,1)S(1)}, u32[]{:S(2)}, u32[]{:S(2)}) collective-permute-start(bf16[4,2,48,640]{3,2,1,0:T(8,128)(2,1)S(1)} %get-tuple-element.139), channel_id=1, source_target_pairs={{0,8},{2,10},{4,12},{6,14},{8,0},{10,2},{12,4},{14,6},{16,24},{18,... | collective-permute-start | bytes 1474568 | tf_op jit(solution)/shard_map/ppermute | solution.py:37
  46.5 23.2 %collective-permute-start.9 = (bf16[4,2,48,640]{3,2,1,0:T(8,128)(2,1)S(1)}, bf16[4,2,48,640]{3,2,1,0:T(8,128)(2,1)S(1)}, u32[]{:S(2)}, u32[]{:S(2)}) collective-permute-start(bf16[4,2,48,640]{3,2,1,0:T(8,128)(2,1)S(1)} %get-tuple-element.139), channel_id=1, source_target_pairs={{0,24},{2,26},{4,28},{6,30},{8,16},{10,18},{12,20},{14,22},{16,8},... | collective-permute-start | bytes 1474568 | tf_op jit(solution)/shard_map/ppermute | solution.py:37
  46.5 25.8 %collective-permute-start.11 = (bf16[2,128,768]{2,1,0:T(8,128)(2,1)S(1)}, bf16[2,128,768]{2,1,0:T(8,128)(2,1)}, u32[]{:S(2)}, u32[]{:S(2)}) collective-permute-start(bf16[2,128,768]{2,1,0:T(8,128)(2,1)S(1)} %copy-done.67), channel_id=1, source_target_pairs={{0,1},{1,0},{2,3},{3,2},{4,5},{5,4},{6,7},{7,6},{8,9},{9,8},{10,11... | collective-permute-start | bytes 1179656 | tf_op jit(solution)/shard_map/ppermute | solution.py:37
  55.4 16.9 %collective-permute-start.10 = (s32[2,384]{1,0:T(2,128)S(1)}, s32[2,384]{1,0:T(2,128)S(1)}, u32[]{:S(2)}, u32[]{:S(2)}) collective-permute-start(s32[2,384]{1,0:T(2,128)S(1)} %pad_add_fusion.7), channel_id=1, source_target_pairs={{0,1},{1,0},{2,3},{3,2},{4,5},{5,4},{6,7},{7,6},{8,9},{9,8},{10,11... | collective-permute-start | bytes 9224 | tf_op jit(solution)/shard_map/ppermute | solution.py:37
  72.4 11.8 %collective-permute-start.13 = (bf16[4,4,2,48,640]{4,3,2,1,0:T(8,128)(2,1)S(1)}, bf16[4,4,2,48,640]{4,3,2,1,0:T(8,128)(2,1)}, u32[]{:S(2)}, u32[]{:S(2)}) collective-permute-start(bf16[4,4,2,48,640]{4,3,2,1,0:T(8,128)(2,1)S(1)} %pad_maximum_fusion.own_ref), channel_id=1, source_target_pairs={{0,2},{2,0},{4,6},{6,4},{8,10},{10,8},{12,14},{14,12},{16,18},{18,... | collective-permute-start | bytes 5898248 | tf_op jit(solution)/shard_map/ppermute | solution.py:37
  257.2 31.0 %collective-permute-start.16 = (bf16[2,768,1024]{2,1,0:T(8,128)(2,1)S(1)}, bf16[2,768,1024]{2,1,0:T(8,128)(2,1)S(1)}, u32[]{:S(2)}, u32[]{:S(2)}) collective-permute-start(bf16[2,768,1024]{2,1,0:T(8,128)(2,1)S(1)} %get-tuple-element.99), channel_id=1, source_target_pairs={{0,2},{2,0},{4,6},{6,4},{8,10},{10,8},{12,14},{14,12},{16,18},{18,... | collective-permute-start | bytes 9437192 | tf_op jit(solution)/shard_map/ppermute | solution.py:37
  257.4 34.3 %collective-permute-start.23 = (bf16[2,768,1024]{2,1,0:T(8,128)(2,1)}, bf16[2,768,1024]{2,1,0:T(8,128)(2,1)S(1)}, u32[]{:S(2)}, u32[]{:S(2)}) collective-permute-start(bf16[2,768,1024]{2,1,0:T(8,128)(2,1)} %get-tuple-element.101), channel_id=1, source_target_pairs={{0,2},{2,0},{4,6},{6,4},{8,10},{10,8},{12,14},{14,12},{16,18},{18,... | collective-permute-start | bytes 9437192 | tf_op jit(solution)/shard_map/ppermute | solution.py:37
  259.6 10.8 %collective-permute-start.15 = (bf16[2,128,768]{2,1,0:T(8,128)(2,1)S(1)}, bf16[2,128,768]{2,1,0:T(8,128)(2,1)S(1)}, u32[]{:S(2)}, u32[]{:S(2)}) collective-permute-start(bf16[2,128,768]{2,1,0:T(8,128)(2,1)S(1)} %slice.337), channel_id=1, source_target_pairs={{0,1},{1,0},{2,3},{3,2},{4,5},{5,4},{6,7},{7,6},{8,9},{9,8},{10,11... | collective-permute-start | bytes 1179656 | tf_op jit(solution)/shard_map/ppermute | solution.py:37
  263.8 23.2 %collective-permute-start.14 = (bf16[2,256,768]{2,1,0:T(8,128)(2,1)S(1)}, bf16[2,256,768]{2,1,0:T(8,128)(2,1)S(1)}, u32[]{:S(2)}, u32[]{:S(2)}) collective-permute-start(bf16[2,256,768]{2,1,0:T(8,128)(2,1)S(1)} %slice.336), channel_id=1, source_target_pairs={{1,0},{3,2},{5,4},{7,6},{9,8},{11,10},{13,12},{15,14},{17,16},{19,... | collective-permute-start | bytes 2359304 | tf_op jit(solution)/shard_map/ppermute | solution.py:735
  289.8 62.2 %collective-permute-start.18 = (bf16[2,4,48,1024]{3,0,2,1:T(2,128)(2,1)S(1)}, bf16[2,4,48,1024]{3,0,2,1:T(2,128)(2,1)S(1)}, u32[]{:S(2)}, u32[]{:S(2)}) collective-permute-start(bf16[2,4,48,1024]{3,0,2,1:T(2,128)(2,1)S(1)} %fusion.22), channel_id=1, source_target_pairs={{0,16},{2,18},{4,20},{6,22},{8,24},{10,26},{12,28},{14,30},{16,0},... | collective-permute-start | bytes 2359304 | tf_op jit(solution)/shard_map/ppermute | solution.py:37
  293.4 21.3 %collective-permute-start.25 = (bf16[2,4,48,1024]{3,0,2,1:T(2,128)(2,1)S(1)}, bf16[2,4,48,1024]{3,0,2,1:T(2,128)(2,1)S(1)}, u32[]{:S(2)}, u32[]{:S(2)}) collective-permute-start(bf16[2,4,48,1024]{3,0,2,1:T(2,128)(2,1)S(1)} %fusion.25), channel_id=1, source_target_pairs={{0,64},{2,66},{4,68},{6,70},{8,72},{10,74},{12,76},{14,78},{16,80}... | collective-permute-start | bytes 2359304 | tf_op jit(solution)/shard_map/ppermute | solution.py:37
  296.8 49.3 %collective-permute-start.24 = (bf16[2,4,48,1024]{3,0,2,1:T(2,128)(2,1)S(1)}, bf16[2,4,48,1024]{3,0,2,1:T(2,128)(2,1)S(1)}, u32[]{:S(2)}, u32[]{:S(2)}) collective-permute-start(bf16[2,4,48,1024]{3,0,2,1:T(2,128)(2,1)S(1)} %fusion.24), channel_id=1, source_target_pairs={{0,32},{2,34},{4,36},{6,38},{8,40},{10,42},{12,44},{14,46},{16,48}... | collective-permute-start | bytes 2359304 | tf_op jit(solution)/shard_map/ppermute | solution.py:37
  298.7 49.3 %collective-permute-start.26 = (bf16[2,4,48,1024]{3,0,2,1:T(2,128)(2,1)S(1)}, bf16[2,4,48,1024]{3,0,2,1:T(2,128)(2,1)S(1)}, u32[]{:S(2)}, u32[]{:S(2)}) collective-permute-start(bf16[2,4,48,1024]{3,0,2,1:T(2,128)(2,1)S(1)} %fusion.26), channel_id=1, source_target_pairs={{0,96},{2,98},{4,100},{6,102},{8,104},{10,106},{12,108},{14,110},{... | collective-permute-start | bytes 2359304 | tf_op jit(solution)/shard_map/ppermute | solution.py:37
  300.7 53.1 %collective-permute-start.17 = (bf16[2,4,48,1024]{3,0,2,1:T(2,128)(2,1)S(1)}, bf16[2,4,48,1024]{3,0,2,1:T(2,128)(2,1)S(1)}, u32[]{:S(2)}, u32[]{:S(2)}) collective-permute-start(bf16[2,4,48,1024]{3,0,2,1:T(2,128)(2,1)S(1)} %fusion.21), channel_id=1, source_target_pairs={{0,8},{2,10},{4,12},{6,14},{8,0},{10,2},{12,4},{14,6},{16,24},{18,... | collective-permute-start | bytes 2359304 | tf_op jit(solution)/shard_map/ppermute | solution.py:37
  314.7 39.2 %collective-permute-start.19 = (bf16[2,4,48,1024]{3,0,2,1:T(2,128)(2,1)S(1)}, bf16[2,4,48,1024]{3,0,2,1:T(2,128)(2,1)S(1)}, u32[]{:S(2)}, u32[]{:S(2)}) collective-permute-start(bf16[2,4,48,1024]{3,0,2,1:T(2,128)(2,1)S(1)} %fusion.23), channel_id=1, source_target_pairs={{0,24},{2,26},{4,28},{6,30},{8,16},{10,18},{12,20},{14,22},{16,8},... | collective-permute-start | bytes 2359304 | tf_op jit(solution)/shard_map/ppermute | solution.py:37
  368.7 13.8 %collective-permute-start.34 = (bf16[2,12,2816]{2,0,1:T(2,128)(2,1)S(1)}, bf16[2,12,2816]{2,0,1:T(2,128)(2,1)S(1)}, u32[]{:S(2)}, u32[]{:S(2)}) collective-permute-start(bf16[2,12,2816]{2,0,1:T(2,128)(2,1)S(1)} %get-tuple-element.157), channel_id=1, source_target_pairs={{0,3},{1,2},{2,1},{3,0},{4,7},{5,6},{6,5},{7,4},{8,11},{9,10},{10,... | collective-permute-start | bytes 405512 | tf_op jit(solution)/shard_map/ppermute | solution.py:343
  374.7 10.7 %collective-permute-start.32 = (bf16[2,12,2816]{2,0,1:T(2,128)(2,1)S(1)}, bf16[2,12,2816]{2,0,1:T(2,128)(2,1)S(1)}, u32[]{:S(2)}, u32[]{:S(2)}) collective-permute-start(bf16[2,12,2816]{2,0,1:T(2,128)(2,1)S(1)} %get-tuple-element.158), channel_id=1, source_target_pairs={{0,5},{1,4},{2,7},{3,6},{4,1},{5,0},{6,3},{7,2},{8,13},{9,12},{10,... | collective-permute-start | bytes 405512 | tf_op jit(solution)/shard_map/ppermute | solution.py:343
  374.7 10.7 %collective-permute-start.31 = (bf16[2,12,2816]{2,0,1:T(2,128)(2,1)S(1)}, bf16[2,12,2816]{2,0,1:T(2,128)(2,1)S(1)}, u32[]{:S(2)}, u32[]{:S(2)}) collective-permute-start(bf16[2,12,2816]{2,0,1:T(2,128)(2,1)S(1)} %get-tuple-element.158), channel_id=1, source_target_pairs={{0,4},{2,6},{4,0},{6,2},{8,12},{10,14},{12,8},{14,10},{16,20},{18,... | collective-permute-start | bytes 405512 | tf_op jit(solution)/shard_map/ppermute | solution.py:37
  376.6 14.8 %collective-permute-start.36 = (bf16[2,12,2816]{2,0,1:T(2,128)(2,1)S(1)}, bf16[2,12,2816]{2,0,1:T(2,128)(2,1)S(1)}, u32[]{:S(2)}, u32[]{:S(2)}) collective-permute-start(bf16[2,12,2816]{2,0,1:T(2,128)(2,1)S(1)} %get-tuple-element.159), channel_id=1, source_target_pairs={{0,7},{1,6},{2,5},{3,4},{4,3},{5,2},{6,1},{7,0},{8,15},{9,14},{10,... | collective-permute-start | bytes 405512 | tf_op jit(solution)/shard_map/ppermute | solution.py:343
  382.9 11.4 %collective-permute-start.37 = (f32[24,320]{1,0:T(8,128)S(1)}, f32[24,320]{1,0:T(8,128)S(1)}, u32[]{:S(2)}, u32[]{:S(2)}) collective-permute-start(f32[24,320]{1,0:T(8,128)S(1)} %select_maximum_fusion), channel_id=1, source_target_pairs={{0,1},{1,0},{2,3},{3,2},{4,5},{5,4},{6,7},{7,6},{8,9},{9,8},{10,11... | collective-permute-start | bytes 92168 | tf_op jit(solution)/shard_map/ppermute | solution.py:37
  (139 other events, 1149.4 us)
Sparse Core Ops, SparseCore 0:
  27.3 120.4 all-gather.2
  213.6 199.3 reduce-scatter.1
